TPU v7x, 128 devices: a whole 4x4x4 slice. The times are simulated.
128 devices in a mesh: dp: 16 (over y_lo, x, core), ctx: 8 (over y_hi, z).
Axes of the slice: x: 4, y: 4 (y_hi: 2, y_lo: 2; y = y_hi * 2 + y_lo), z: 4, core: 2. Of those that a mesh axis runs over, the one named last changes fastest.
Arguments:
- tokens: bfloat16 [32, 1024, 4096], P('dp', 'ctx'), may hold values from -6 to 6
- queries: bfloat16 [32, 1024, 4096], P('dp', 'ctx'), may hold values from -6 to 6
- out_grad: bfloat16 [32, 1024, 4096], P('dp', 'ctx'), may hold values from -6 to 6
- kv_weight: bfloat16 [4096, 1024], replicated, may hold values from -0.09375 to 0.09375
- doc_lengths: int32 [32, 8], P('dp'), may hold values from 1 to 640, 1024 in all within a row
- swap_plan: int32 [16, 8, 3], P('dp', 'ctx'), may hold values from 0 to 1
Outputs:
- query_grad: bfloat16 [32, 1024, 4096], P('dp', 'ctx')
- weight_grad: float32 [4096, 1024], P(('dp', 'ctx'))
Inputs may be any that keep to these rules, and one draw needn't show every extreme that they name: `doc_lengths`: each row sums to 1024; its longest document has exactly 640 tokens. `swap_plan`: entry r names, among the device's pages (sequence first, then page order), the one traded in round r.
All inputs are finite; a program needn't handle non-finite values.
Results may differ from a plain program's by a relative error of at most 0.014.
Values may be sent and summed in bfloat16 or wider, within the bound.
No kernel may reach another device: no remote copies, remote signals or barrier semaphores. Data moves between devices by JAX's collectives and lax.ppermute only.
A program may use at most 256 MiB of HBM per device.

v0:
```python
import jax
import jax.numpy as jnp
from jax import lax
from jax.sharding import PartitionSpec as P

HEAD = 128
ROUNDS = 3


def partner(block, axis, stride):
    count = lax.axis_size(axis)
    route = []
    for low in range(count):
        high = low | 1 << stride
        if high != low and high < count:
            route += [(low, high), (high, low)]
    return lax.ppermute(block, axis, route)


def trade(pages, select, incoming):
    mask = (jnp.arange(pages.shape[0], dtype=jnp.int32) == select)[:, None, None]
    return jnp.where(mask, incoming[None], pages)


def per_device(tokens, queries, out_grad, kv_weight, doc_lengths, swap_plan):
    seqs, tok_rows, width = tokens.shape
    qwidth = queries.shape[2]
    kv_pair = kv_weight.shape[1]
    kv_cols = kv_pair // 2
    group_count = kv_cols // HEAD
    heads_per = qwidth // kv_cols
    scale = HEAD ** (-0.5)
    moving = (tokens, queries, out_grad)
    for step in range(ROUNDS):
        select = swap_plan[0, 0, step]
        outgoing = [lax.dynamic_index_in_dim(piece, select, 0, keepdims=False) for piece in moving]
        received = partner((outgoing[0], outgoing[1], outgoing[2]), "dp", step)
        moving = tuple((trade(moving[index], select, received[index]) for index in range(3)))
    moved_queries = moving[1]
    moved_grad = moving[2]
    moved_tokens = moving[0]
    kv_rows = jnp.dot(
        moved_tokens.reshape(-1, width), kv_weight, preferred_element_type=jnp.float32
    )
    kv_rows = kv_rows.astype(jnp.bfloat16).reshape(seqs, tok_rows, kv_pair)
    kv_whole = lax.all_gather(kv_rows, "ctx", axis=1, tiled=True)
    seq_len = kv_whole.shape[1]
    query_pos = lax.axis_index("ctx") * tok_rows + jnp.arange(tok_rows, dtype=jnp.int32)
    key_pos = jnp.arange(seq_len, dtype=jnp.int32)
    ends = jnp.cumsum(doc_lengths, axis=1)
    query_doc = jnp.sum((query_pos[None, :, None] >= ends[:, None, :]).astype(jnp.int32), axis=2)
    key_doc = jnp.sum((key_pos[None, :, None] >= ends[:, None, :]).astype(jnp.int32), axis=2)
    allowed = (query_doc[:, :, None] == key_doc[:, None, :]) & (
        key_pos[None, None, :] <= query_pos[None, :, None]
    )
    allowed = allowed[:, None]
    dq_parts = []
    dk_parts = []
    dv_parts = []
    for group in range(group_count):
        lo = group * heads_per * HEAD
        hi = lo + heads_per * HEAD
        q_group = moved_queries[:, :, lo:hi].reshape(seqs, tok_rows, heads_per, HEAD)
        d_group = moved_grad[:, :, lo:hi].reshape(seqs, tok_rows, heads_per, HEAD)
        k_group = kv_whole[:, :, group * HEAD : (group + 1) * HEAD]
        v_group = kv_whole[:, :, kv_cols + group * HEAD : kv_cols + (group + 1) * HEAD]
        scores = (
            jnp.einsum("bthd,bud->bhtu", q_group, k_group, preferred_element_type=jnp.float32)
            * scale
        )
        weights = jnp.where(allowed, jnp.exp(scores), 0.0)
        probs = weights / jnp.sum(weights, axis=-1, keepdims=True)
        probs_low = probs.astype(jnp.bfloat16)
        dprobs = jnp.einsum("bthd,bud->bhtu", d_group, v_group, preferred_element_type=jnp.float32)
        delta = jnp.sum(probs * dprobs, axis=-1, keepdims=True)
        dscores = (probs * (dprobs - delta) * scale).astype(jnp.bfloat16)
        dq_group = jnp.einsum(
            "bhtu,bud->bthd", dscores, k_group, preferred_element_type=jnp.float32
        )
        dq_parts.append(dq_group.reshape(seqs, tok_rows, heads_per * HEAD).astype(jnp.bfloat16))
        dk_parts.append(
            jnp.einsum("bhtu,bthd->bud", dscores, q_group, preferred_element_type=jnp.float32)
        )
        dv_parts.append(
            jnp.einsum("bhtu,bthd->bud", probs_low, d_group, preferred_element_type=jnp.float32)
        )
    query_grad = jnp.concatenate(dq_parts, axis=2)
    kv_terms = jnp.concatenate(dk_parts + dv_parts, axis=2)
    kv_grad = lax.psum_scatter(
        kv_terms.astype(jnp.bfloat16), "ctx", scatter_dimension=1, tiled=True
    )
    flat_sources = moved_tokens.reshape(-1, width)
    flat_grad = kv_grad.reshape(-1, kv_pair)
    piece = flat_sources
    weight_grad = lax.psum_scatter(
        lax.dot_general(
            piece, flat_grad, (((0,), (0,)), ((), ())), preferred_element_type=jnp.float32
        ),
        ("dp", "ctx"),
        scatter_dimension=0,
        tiled=True,
    )
    return (query_grad, weight_grad)


def solution(mesh):
    in_specs = (
        P("dp", "ctx", None),
        P("dp", "ctx", None),
        P("dp", "ctx", None),
        P(),
        P("dp", None),
        P("dp", "ctx", None),
    )
    out_specs = (P("dp", "ctx", None), P(("dp", "ctx"), None))
    return jax.shard_map(
        per_device, mesh=mesh, in_specs=in_specs, out_specs=out_specs, check_vma=False
    )
```

profile of v0, /device:TPU:0, one launch (start us, length us, event | category | flops | bytes accessed | tf_op | source)
XLA Modules:
  0.0 1157.3 jit_solution(13409304293616685195)
XLA Ops:
  34.1 17.7 %collective-permute-done.4 = bf16[128,4096]{1,0:T(8,128)(2,1)S(1)} collective-permute-done((bf16[128,4096]{1,0:T(8,128)(2,1)}, bf16[128,4096]{1,0:T(8,128)(2,1)S(1)}, u32[]{:S(2)}, u32[]{:S(2)}) %collective-permute-start.4) | collective-permute-done | bytes 1048608 | tf_op jit(solution)/shard_map/ppermute | solution.py:17
  51.8 22.6 %collective-permute-done.7 = bf16[128,4096]{1,0:T(8,128)(2,1)} collective-permute-done((bf16[128,4096]{1,0:T(8,128)(2,1)}, bf16[128,4096]{1,0:T(8,128)(2,1)}, u32[]{:S(2)}, u32[]{:S(2)}) %collective-permute-start.7) | collective-permute-done | bytes 1048608 | tf_op jit(solution)/shard_map/ppermute | solution.py:17
  74.4 22.1 %collective-permute-done.1 = bf16[128,4096]{1,0:T(8,128)(2,1)} collective-permute-done((bf16[128,4096]{1,0:T(8,128)(2,1)}, bf16[128,4096]{1,0:T(8,128)(2,1)}, u32[]{:S(2)}, u32[]{:S(2)}) %collective-permute-start.1) | collective-permute-done | bytes 1048608 | tf_op jit(solution)/shard_map/ppermute | solution.py:17
  107.5 19.9 %collective-permute-done.5 = bf16[128,4096]{1,0:T(8,128)(2,1)S(1)} collective-permute-done((bf16[128,4096]{1,0:T(8,128)(2,1)S(1)}, bf16[128,4096]{1,0:T(8,128)(2,1)S(1)}, u32[]{:S(2)}, u32[]{:S(2)}) %collective-permute-start.5) | collective-permute-done | bytes 1048608 | tf_op jit(solution)/shard_map/ppermute | solution.py:17
  127.4 22.5 %collective-permute-done.8 = bf16[128,4096]{1,0:T(8,128)(2,1)S(1)} collective-permute-done((bf16[128,4096]{1,0:T(8,128)(2,1)S(1)}, bf16[128,4096]{1,0:T(8,128)(2,1)S(1)}, u32[]{:S(2)}, u32[]{:S(2)}) %collective-permute-start.8) | collective-permute-done | bytes 1048608 | tf_op jit(solution)/shard_map/ppermute | solution.py:17
  149.9 21.2 %collective-permute-done.2 = bf16[128,4096]{1,0:T(8,128)(2,1)S(1)} collective-permute-done((bf16[128,4096]{1,0:T(8,128)(2,1)S(1)}, bf16[128,4096]{1,0:T(8,128)(2,1)S(1)}, u32[]{:S(2)}, u32[]{:S(2)}) %collective-permute-start.2) | collective-permute-done | bytes 1048608 | tf_op jit(solution)/shard_map/ppermute | solution.py:17
  196.1 54.7 %all-gather.2.cloned.1.call-done = bf16[2,1024,1024]{2,1,0:T(8,128)(2,1)} async-done(((bf16[2,128,1024]{2,1,0:T(8,128)(2,1)}), bf16[2,1024,1024]{2,1,0:T(8,128)(2,1)}) %all-gather.2.cloned.1.call-update) | async-done | bytes 4194320 | tf_op jit(solution)/shard_map/all_gather | solution.py:46
  250.8 5.7 fusion.104
  261.8 6.0 fusion.99
  267.8 10.3 fusion.17
  278.1 14.6 %fusion.67 = bf16[2,1024,1024]{1,2,0:T(8,128)(2,1)} fusion(bf16[2,128,8,128]{1,3,2,0:T(8,128)(2,1)} %bitcast.458, f32[2,1024,128,8]{2,1,3,0:T(8,128)} %fusion.99, f32[2,1024,128,8]{2,1,3,0:T(8,128)} %get-tuple-element.26, f32[2,8,128]{2,1,0:T(8,128)S(1)} %get-tuple-element.2, pred[2,128,1024]{1,2,0:T(8,128)(4,1)S(1)} %compare_and_fusion), kind=kOutput, calls=%fused_computation.83 | convolution fusion | flops 560204800 | bytes 35143680 | tf_op jit(solution)/shard_map/bhtu,bthd->bud/dot_general | solution.py:82
  298.3 14.4 %fusion.66 = bf16[2,1024,1024]{1,2,0:T(8,128)(2,1)} fusion(bf16[2,1024,1024]{1,2,0:T(8,128)(2,1)} %fusion.67, bf16[2,128,8,128]{1,3,2,0:T(8,128)(2,1)} %bitcast.454, f32[2,1024,128,8]{2,1,3,0:T(8,128)} %fusion.98, f32[2,1024,128,8]{2,1,3,0:T(8,128)} %copy-done, f32[2,8,128]{2,1,0:T(8,128)S(1)} %get-tuple-element.3, ...), kind=kOutput, calls=%fused_computation.82 | convolution fusion | flops 560204800 | bytes 35143680 | tf_op jit(solution)/shard_map/bhtu,bthd->bud/dot_general | solution.py:82
  318.2 14.4 %fusion.65 = bf16[2,1024,1024]{1,2,0:T(8,128)(2,1)} fusion(bf16[2,1024,1024]{1,2,0:T(8,128)(2,1)} %fusion.66, bf16[2,128,8,128]{1,3,2,0:T(8,128)(2,1)} %bitcast.450, f32[2,1024,128,8]{2,1,3,0:T(8,128)} %fusion.97, f32[2,1024,128,8]{2,1,3,0:T(8,128)} %copy-done.1, f32[2,8,128]{2,1,0:T(8,128)S(1)} %get-tuple-element.4, ...), kind=kOutput, calls=%fused_computation.81 | convolution fusion | flops 560204800 | bytes 35143680 | tf_op jit(solution)/shard_map/bhtu,bthd->bud/dot_general | solution.py:82
  338.2 14.6 %fusion.64 = bf16[2,1024,1024]{1,2,0:T(8,128)(2,1)} fusion(bf16[2,1024,1024]{1,2,0:T(8,128)(2,1)} %fusion.65, bf16[2,128,8,128]{1,3,2,0:T(8,128)(2,1)} %bitcast.447, f32[2,1024,128,8]{2,1,3,0:T(8,128)} %fusion.96, f32[2,1024,128,8]{2,1,3,0:T(8,128)} %fusion.104, f32[2,8,128]{2,1,0:T(8,128)S(1)} %get-tuple-element.5, ...), kind=kOutput, calls=%fused_computation.80 | convolution fusion | flops 560204800 | bytes 35143680 | tf_op jit(solution)/shard_map/bhtu,bthd->bud/dot_general | solution.py:82
  352.8 6.5 fusion.89
  359.4 6.5 fusion.83
  372.0 11.3 copy.208
  388.9 82.6 %reduce-scatter.7.cloned.1.call-done = bf16[128,2048]{1,0:T(8,128)(2,1)} async-done(((bf16[1024,2048]{1,0:T(8,128)(2,1)}), bf16[128,2048]{1,0:T(8,128)(2,1)}) %reduce-scatter.7.cloned.1.call-update) | async-done | bytes 524304
  472.9 8.1 convolution_bitcast_fusion
  481.1 13.9 %fusion.92 = bf16[2,128,8,128]{3,1,2,0:T(8,128)(2,1)S(1)} fusion(f32[2,1024,128,8]{2,1,3,0:T(8,128)} %fusion.96, bf16[2,1024,1024]{2,1,0:T(8,128)(2,1)} %all-gather.2.cloned.1.call-done, f32[2,1024,128,8]{2,1,3,0:T(8,128)} %fusion.104, f32[2,8,128]{2,1,0:T(8,128)S(1)} %get-tuple-element.5, pred[2,128,1024]{1,2,0:T(8,128)(4,1)S(1)} %compare_and_fusion), kind=kOutput, calls=%fused_computation.92 | convolution fusion | flops 560204800 | bytes 35143680 | tf_op jit(solution)/shard_map/bhtu,bud->bthd/dot_general | solution.py:77
  495.2 13.6 %fusion.93 = bf16[2,128,8,128]{3,1,2,0:T(8,128)(2,1)S(1)} fusion(f32[2,1024,128,8]{2,1,3,0:T(8,128)} %fusion.97, bf16[2,1024,1024]{2,1,0:T(8,128)(2,1)} %all-gather.2.cloned.1.call-done, f32[2,1024,128,8]{2,1,3,0:T(8,128)} %copy-done.1, f32[2,8,128]{2,1,0:T(8,128)S(1)} %get-tuple-element.4, pred[2,128,1024]{1,2,0:T(8,128)(4,1)S(1)} %compare_and_fusion), kind=kOutput, calls=%fused_computation.93 | convolution fusion | flops 560204800 | bytes 35143680 | tf_op jit(solution)/shard_map/bhtu,bud->bthd/dot_general | solution.py:77
  509.0 13.6 %fusion.94 = bf16[2,128,8,128]{3,1,2,0:T(8,128)(2,1)S(1)} fusion(f32[2,1024,128,8]{2,1,3,0:T(8,128)} %fusion.98, bf16[2,1024,1024]{2,1,0:T(8,128)(2,1)} %all-gather.2.cloned.1.call-done, f32[2,1024,128,8]{2,1,3,0:T(8,128)} %copy-done, f32[2,8,128]{2,1,0:T(8,128)S(1)} %get-tuple-element.3, pred[2,128,1024]{1,2,0:T(8,128)(4,1)S(1)} %compare_and_fusion), kind=kOutput, calls=%fused_computation.94 | convolution fusion | flops 560204800 | bytes 35143680 | tf_op jit(solution)/shard_map/bhtu,bud->bthd/dot_general | solution.py:77
  522.9 13.6 %fusion.95 = bf16[2,128,8,128]{3,1,2,0:T(8,128)(2,1)S(1)} fusion(f32[2,1024,128,8]{2,1,3,0:T(8,128)} %fusion.99, bf16[2,1024,1024]{2,1,0:T(8,128)(2,1)} %all-gather.2.cloned.1.call-done, f32[2,1024,128,8]{2,1,3,0:T(8,128)} %get-tuple-element.26, f32[2,8,128]{2,1,0:T(8,128)S(1)} %get-tuple-element.2, pred[2,128,1024]{1,2,0:T(8,128)(4,1)S(1)} %compare_and_fusion), kind=kOutput, calls=%fused_computation.95 | convolution fusion | flops 560204800 | bytes 35143680 | tf_op jit(solution)/shard_map/bhtu,bud->bthd/dot_general | solution.py:77
  538.2 612.1 %reduce-scatter.5.cloned.1.call-done = f32[32,1024]{1,0:T(8,128)} async-done(((f32[4096,1024]{1,0:T(8,128)}), f32[32,1024]{1,0:T(8,128)}) %reduce-scatter.5.cloned.1.call-update) | async-done | bytes 131088 | tf_op jit(solution)/shard_map/reduce_scatter | solution.py:95
  (101 shorter events, 94.3 us)
Async XLA Ops:
  7.2 243.7 %all-gather.2.cloned.1.call-start = ((), (), s32[]{:S(2)}) async-start(), calls=%async_computation.2 | async-start | bytes 4718592 | tf_op jit(solution)/shard_map/all_gather | solution.py:46
  11.8 7.9 collective-permute-start.3
  14.2 5.5 collective-permute-start.6
  17.0 3.7 collective-permute-start
  24.5 4.3 copy-start.3
  25.7 26.2 %collective-permute-start.4 = (bf16[128,4096]{1,0:T(8,128)(2,1)}, bf16[128,4096]{1,0:T(8,128)(2,1)S(1)}, u32[]{:S(2)}, u32[]{:S(2)}) collective-permute-start(bf16[128,4096]{1,0:T(8,128)(2,1)} %dynamic-slice_bitcast_fusion.4), channel_id=1, source_target_pairs={{0,16},{16,0},{8,24},{24,8},{32,48},{48,32},{40,56},{56,40},{64,80... | collective-permute-start | bytes 3145736 | tf_op jit(solution)/shard_map/ppermute | solution.py:17
  28.4 46.1 %collective-permute-start.7 = (bf16[128,4096]{1,0:T(8,128)(2,1)}, bf16[128,4096]{1,0:T(8,128)(2,1)}, u32[]{:S(2)}, u32[]{:S(2)}) collective-permute-start(bf16[128,4096]{1,0:T(8,128)(2,1)} %dynamic-slice_bitcast_fusion.1), channel_id=1, source_target_pairs={{0,16},{16,0},{8,24},{24,8},{32,48},{48,32},{40,56},{56,40},{64,80... | collective-permute-start | bytes 3145736 | tf_op jit(solution)/shard_map/ppermute | solution.py:17
  29.9 66.6 %collective-permute-start.1 = (bf16[128,4096]{1,0:T(8,128)(2,1)}, bf16[128,4096]{1,0:T(8,128)(2,1)}, u32[]{:S(2)}, u32[]{:S(2)}) collective-permute-start(bf16[128,4096]{1,0:T(8,128)(2,1)} %dynamic-slice_bitcast_fusion.7), channel_id=1, source_target_pairs={{0,16},{16,0},{8,24},{24,8},{32,48},{48,32},{40,56},{56,40},{64,80... | collective-permute-start | bytes 3145736 | tf_op jit(solution)/shard_map/ppermute | solution.py:17
  99.8 27.6 %collective-permute-start.5 = (bf16[128,4096]{1,0:T(8,128)(2,1)S(1)}, bf16[128,4096]{1,0:T(8,128)(2,1)S(1)}, u32[]{:S(2)}, u32[]{:S(2)}) collective-permute-start(bf16[128,4096]{1,0:T(8,128)(2,1)S(1)} %dynamic-slice_bitcast_fusion.3), channel_id=1, source_target_pairs={{0,32},{32,0},{8,40},{40,8},{16,48},{48,16},{24,56},{56,24},{64,96... | collective-permute-start | bytes 3145736 | tf_op jit(solution)/shard_map/ppermute | solution.py:17
  103.0 46.9 %collective-permute-start.8 = (bf16[128,4096]{1,0:T(8,128)(2,1)S(1)}, bf16[128,4096]{1,0:T(8,128)(2,1)S(1)}, u32[]{:S(2)}, u32[]{:S(2)}) collective-permute-start(bf16[128,4096]{1,0:T(8,128)(2,1)S(1)} %dynamic-slice_bitcast_fusion), channel_id=1, source_target_pairs={{0,32},{32,0},{8,40},{40,8},{16,48},{48,16},{24,56},{56,24},{64,96... | collective-permute-start | bytes 3145736 | tf_op jit(solution)/shard_map/ppermute | solution.py:17
  103.6 69.9 %slice-start.4 = ((s8[8388608]{0:T(1024)(128)(4,1)}), s8[4194304]{0:T(1024)(128)(4,1)S(1)}, s32[]{:S(2)}) async-start(s8[8388608]{0:T(1024)(128)(4,1)} %bitcast.464), calls=%async_computation.9 | async-start | bytes 8388608
  103.6 67.4 %collective-permute-start.2 = (bf16[128,4096]{1,0:T(8,128)(2,1)S(1)}, bf16[128,4096]{1,0:T(8,128)(2,1)S(1)}, u32[]{:S(2)}, u32[]{:S(2)}) collective-permute-start(bf16[128,4096]{1,0:T(8,128)(2,1)S(1)} %dynamic-slice_bitcast_fusion.6), channel_id=1, source_target_pairs={{0,32},{32,0},{8,40},{40,8},{16,48},{48,16},{24,56},{56,24},{64,96... | collective-permute-start | bytes 3145736 | tf_op jit(solution)/shard_map/ppermute | solution.py:17
  107.5 66.0 %slice-start.5 = ((s8[8388608]{0:T(1024)(128)(4,1)}), s8[4194304]{0:T(1024)(128)(4,1)S(1)}, s32[]{:S(2)}) async-start(s8[8388608]{0:T(1024)(128)(4,1)} %bitcast.464), calls=%async_computation.10 | async-start | bytes 8388608
  173.5 3.7 copy-start.10
  176.6 294.9 %reduce-scatter.7.cloned.1.call-start = ((), (), s32[]{:S(2)}) async-start(), calls=%async_computation.4 | async-start | bytes 4718592
  250.8 5.7 copy-start.7
  258.9 8.9 copy-start
  261.8 16.3 %copy-start.1 = (f32[2,1024,128,8]{2,1,3,0:T(8,128)}, f32[2,1024,128,8]{2,1,3,0:T(8,128)S(1)}, u32[]{:S(2)}) copy-start(f32[2,1024,128,8]{2,1,3,0:T(8,128)S(1)} %fusion.103) | copy-start | bytes 25165828
  261.8 6.1 copy-start.9
  352.8 6.6 copy-start.4
  352.8 13.1 %slice-start = ((s8[8388608]{0:T(1024)(128)(4,1)}), s8[4194304]{0:T(1024)(128)(4,1)S(1)}, s32[]{:S(2)}) async-start(s8[8388608]{0:T(1024)(128)(4,1)} %bitcast.435), calls=%async_computation.5 | async-start | bytes 8388608
  359.4 6.5 slice-start.1
  359.4 9.6 slice-start.2
  388.9 761.5 %reduce-scatter.5.cloned.1.call-start = ((), (), s32[]{:S(2)}) async-start(), calls=%async_computation.3 | async-start | bytes 16908288 | tf_op jit(solution)/shard_map/reduce_scatter | solution.py:95
  (5 other events, 12.0 us)
Sparse Core Ops, SparseCore 0:
  176.8 74.0 all-gather.1
  389.0 82.4 reduce-scatter.6
  481.2 669.1 reduce-scatter.4
where the time goes:
time: 1160 us
  waiting for transfers between devices  875 us (75%)
  matrix products  187 us (16%)
  local copies, waits for them, and re-layouts  49.1 us (4%)
  between operations  20.4 us (2%)
  other arithmetic  13.7 us (1%)
  starting transfers between devices  11.7 us (1%)
    reduce_scatter x1, waiting for transfers between devices, per_device(): lax.psum_scatter(lax.dot_general(piece, flat_grad, (((0,), (0,)), ((), ()...  612 us
    ppermute x9, waiting for transfers between devices, partner(): return lax.ppermute(block, axis, route)  126 us
    unnamed x4, waiting for transfers between devices  82.6 us
    dot_general x4, matrix products, per_device(): jnp.einsum('bhtu,bthd->bud', dscores, q_group, preferred_element_type=jnp...  58 us
    dot_general x4, matrix products, per_device(): jnp.einsum('bhtu,bud->bthd', dscores, k_group, preferred_element_type=jnp...  54.8 us
    all_gather x1, waiting for transfers between devices, per_device(): kv_whole = lax.all_gather(kv_rows, 'ctx', axis=1, tiled=True)  54.7 us
  transfers between devices with their start and end apart: 12, of which 9 were waited for; matrix products, arithmetic and copies ran while one was open for 7% of the time, Pallas kernels for 0%

commit v1 on v0

v1 whole, which is shorter than its diff:
```python
import functools

import jax
import jax.numpy as jnp
from jax import lax
from jax.experimental import pallas as pl
from jax.experimental.pallas import tpu as pltpu
from jax.sharding import PartitionSpec as P

HEAD = 128
ROUNDS = 3
AXES = ("dp", "ctx")
N_DP = 16
N_CTX = 8
TEAM = 8
WINDOW = 6
BLOCK = 128
GROUPS = 4
MASKED = -1e30
LOG2E = 1.4426950408889634


def move(value, target):
    route = []
    for dp in range(N_DP):
        for ctx in range(N_CTX):
            to_dp, to_ctx = target(dp, ctx)
            if 0 <= to_ctx < N_CTX:
                route.append((dp * N_CTX + ctx, to_dp * N_CTX + to_ctx))
    return lax.ppermute(value, AXES, route)


def flip_dp(bits):
    return lambda dp, ctx: (dp ^ bits, ctx)


def flip_ctx(bits):
    return lambda dp, ctx: (dp, ctx ^ bits)


def shift_ctx(by):
    return lambda dp, ctx: (dp, ctx + by)


def flip_y(low, high):
    return lambda dp, ctx: (dp ^ (low * 8), ctx ^ (high * 4))


def trade(pages, plan):
    for step in range(ROUNDS):
        outgoing = lax.dynamic_index_in_dim(pages, plan[step], 0, keepdims=False)
        incoming = move(outgoing, flip_dp(1 << step))
        mask = jnp.arange(2, dtype=jnp.int32) == plan[step]
        mask = mask.reshape((2,) + (1,) * (pages.ndim - 1))
        pages = jnp.where(mask, incoming[None], pages)
    return pages


def attention_kernel(
    first_ref, q_ref, d_ref, k_ref, v_ref, start_ref,
    dq_ref, part_ref,
    q_s, d_s, w_s, dp_s, acc_s,
):
    row = pl.program_id(0)
    first = first_ref[row]
    heads = q_ref.shape[-1] // HEAD
    queries = heads * BLOCK
    scale = HEAD ** (-0.5)
    for head in range(heads):
        at = slice(head * HEAD, (head + 1) * HEAD)
        q_s[head * BLOCK : (head + 1) * BLOCK, :] = q_ref[0, 0, :, at]
        d_s[head * BLOCK : (head + 1) * BLOCK, :] = d_ref[0, 0, :, at]
    start = start_ref[0]
    key_iota = lax.broadcasted_iota(jnp.int32, (BLOCK, BLOCK), 0)
    query_iota = lax.broadcasted_iota(jnp.int32, (BLOCK, BLOCK), 1) + (WINDOW - 1) * BLOCK
    nt = (((1,), (1,)), ((), ()))
    nn = (((1,), (0,)), ((), ()))

    def forward(index, carry):
        total, dot = carry
        at = pl.ds(pl.multiple_of(index * BLOCK, BLOCK), BLOCK)
        key_pos = key_iota + index * BLOCK
        seen = (key_pos >= start) & (key_pos <= query_iota)
        bias = jnp.where(seen, 0.0, MASKED)
        bias = jnp.concatenate([bias] * heads, axis=1)
        scores = lax.dot_general(k_ref[0, at, :], q_s[...], nt, preferred_element_type=jnp.float32)
        weights = jnp.exp2(scores * (scale * LOG2E) + bias)
        dprobs = lax.dot_general(v_ref[0, at, :], d_s[...], nt, preferred_element_type=jnp.float32)
        w_s[at, :] = weights
        dp_s[at, :] = dprobs
        total = total + jnp.sum(weights, axis=0, keepdims=True)
        dot = dot + jnp.sum(weights * dprobs, axis=0, keepdims=True)
        return total, dot

    zero = jnp.zeros((1, queries), jnp.float32)
    total, dot = lax.fori_loop(first, WINDOW, forward, (zero, zero))
    inverse = 1.0 / total
    delta = dot * inverse
    acc_s[...] = jnp.zeros_like(acc_s)

    def skip(index, carry):
        part_ref[index, 0] = jnp.zeros(part_ref.shape[2:], part_ref.dtype)
        return carry

    lax.fori_loop(0, first, skip, 0)

    def backward(index, carry):
        at = pl.ds(pl.multiple_of(index * BLOCK, BLOCK), BLOCK)
        probs = w_s[at, :] * inverse
        dscores = (probs * (dp_s[at, :] - delta) * scale).astype(jnp.bfloat16)
        dv = lax.dot_general(
            probs.astype(jnp.bfloat16), d_s[...], nn, preferred_element_type=jnp.float32
        )
        dk = lax.dot_general(dscores, q_s[...], nn, preferred_element_type=jnp.float32)
        part_ref[index, 0, :, :HEAD] = dk.astype(part_ref.dtype)
        part_ref[index, 0, :, HEAD:] = dv.astype(part_ref.dtype)
        acc_s[...] += lax.dot_general(
            k_ref[0, at, :], dscores, (((0,), (0,)), ((), ())), preferred_element_type=jnp.float32
        )
        return carry

    lax.fori_loop(first, WINDOW, backward, 0)
    for head in range(heads):
        at = slice(head * HEAD, (head + 1) * HEAD)
        dq_ref[0, :, at] = acc_s[:, head * BLOCK : (head + 1) * BLOCK].T.astype(dq_ref.dtype)


def attention(first, pages, window, start, group):
    rows, _, toks, width = pages.shape
    keys = window.shape[1]
    queries = width // HEAD * toks
    pairs = rows * queries * keys
    spec = pltpu.PrefetchScalarGridSpec(
        num_scalar_prefetch=1,
        grid=(rows,),
        in_specs=[
            pl.BlockSpec((1, 1, toks, width), lambda b, f: (b, 0, 0, 0)),
            pl.BlockSpec((1, 1, toks, width), lambda b, f: (b, 1, 0, 0)),
            pl.BlockSpec((1, keys, HEAD), lambda b, f: (b, 0, group)),
            pl.BlockSpec((1, keys, HEAD), lambda b, f: (b, 0, GROUPS + group)),
            pl.BlockSpec((1, 1, toks), lambda b, f: (b, 0, 0)),
        ],
        out_specs=[
            pl.BlockSpec((1, toks, width), lambda b, f: (b, 0, 0)),
            pl.BlockSpec((WINDOW, 1, BLOCK, 2 * HEAD), lambda b, f: (0, b, 0, 0)),
        ],
        scratch_shapes=[
            pltpu.VMEM((queries, HEAD), jnp.bfloat16),
            pltpu.VMEM((queries, HEAD), jnp.bfloat16),
            pltpu.VMEM((keys, queries), jnp.float32),
            pltpu.VMEM((keys, queries), jnp.float32),
            pltpu.VMEM((HEAD, queries), jnp.float32),
        ],
    )
    return pl.pallas_call(
        attention_kernel,
        grid_spec=spec,
        out_shape=[
            jax.ShapeDtypeStruct((rows, toks, width), jnp.bfloat16),
            jax.ShapeDtypeStruct((WINDOW, rows, BLOCK, 2 * HEAD), jnp.bfloat16),
        ],
        compiler_params=pltpu.CompilerParams(vmem_limit_bytes=32 * 1024 * 1024),
        cost_estimate=pl.CostEstimate(
            flops=10 * pairs * HEAD, bytes_accessed=8 * 1024 * 1024, transcendentals=pairs
        ),
    )(first, pages, pages, window, window, start)


def origins(plan_all, me):
    ranks = jnp.arange(TEAM, dtype=jnp.int32)
    table = ranks[:, None] * 2 + jnp.arange(2, dtype=jnp.int32)[None, :]
    for step in range(ROUNDS):
        select = plan_all[:, step]
        taken = jnp.where(select == 0, table[:, 0], table[:, 1])
        low = 1 << step
        swapped = jnp.flip(taken.reshape(TEAM // (2 * low), 2, low), axis=1).reshape(TEAM)
        table = jnp.where(
            jnp.arange(2, dtype=jnp.int32)[None, :] == select[:, None], swapped[:, None], table
        )
    return table


def per_device(tokens, queries, out_grad, kv_weight, doc_lengths, swap_plan):
    seqs, toks, width = tokens.shape
    pair = kv_weight.shape[1]
    cols = pair // 2
    group_width = queries.shape[2] // GROUPS
    dp = lax.axis_index("dp")
    ctx = lax.axis_index("ctx")
    team_rank = lax.rem(dp, TEAM)
    plan = swap_plan[0, 0]

    flat = tokens.reshape(seqs * toks, width)
    kv_own = jnp.dot(flat, kv_weight, preferred_element_type=jnp.float32).astype(jnp.bfloat16)
    kv_moved = trade(kv_own.reshape(seqs, toks, pair), plan)
    arrived = [move(kv_moved, shift_ctx(by)) for by in range(WINDOW - 1, 0, -1)]
    window = jnp.concatenate(arrived + [kv_moved], axis=1)

    ends = jnp.cumsum(doc_lengths, axis=1)
    pos = ctx * toks + jnp.arange(toks, dtype=jnp.int32)
    begun = jnp.max(
        jnp.where(ends[:, None, :] <= pos[None, :, None], ends[:, None, :], 0), axis=2
    )
    start = begun - (ctx - (WINDOW - 1)) * toks
    first = start[:, 0] // BLOCK
    start = start[:, None, :]

    moved = []
    for group in range(GROUPS):
        at = slice(group * group_width, (group + 1) * group_width)
        moved.append(trade(jnp.stack([queries[:, :, at], out_grad[:, :, at]], axis=1), plan))

    plans = plan[None]
    for step in range(ROUNDS):
        other = move(plans, flip_dp(1 << step))
        plans = jnp.concatenate([plans, other], axis=0)
    ranks = jnp.arange(TEAM, dtype=jnp.int32)
    plan_all = plans[ranks ^ team_rank]
    table = origins(plan_all, team_rank)
    part = width // (2 * TEAM)

    def columns(rank):
        return jnp.concatenate(
            [
                lax.dynamic_slice_in_dim(flat, rank * part, part, 1),
                lax.dynamic_slice_in_dim(flat, width // 2 + rank * part, part, 1),
            ],
            axis=1,
        )

    sources = [columns(team_rank)]
    sources += [move(columns(team_rank ^ bits), flip_dp(bits)) for bits in range(1, TEAM)]
    sources = jnp.stack(sources).reshape(TEAM * seqs, toks, 2 * part)
    ordered = []
    for bits in range(TEAM):
        for slot in range(seqs):
            origin = table[team_rank ^ bits, slot]
            place = ((origin // 2) ^ team_rank) * 2 + origin % 2
            ordered.append(lax.dynamic_index_in_dim(sources, place, 0, keepdims=False))
    ordered = jnp.concatenate(ordered, axis=0)

    z = lax.rem(ctx, 4)
    y_high = ctx // 4
    y_low = dp // TEAM
    query_parts = []
    grad_parts = []
    for group in range(GROUPS):
        query_grad, kv_part = attention(first, moved[group], window, start, group)
        query_parts.append(query_grad)
        total = kv_part[WINDOW - 1].astype(jnp.float32)
        for by in range(1, WINDOW):
            total = total + move(kv_part[WINDOW - 1 - by], shift_ctx(-by)).astype(jnp.float32)
        kv_grad = total.astype(jnp.bfloat16)
        chips = jnp.stack([kv_grad] + [move(kv_grad, flip_dp(2 * k)) for k in range(1, 4)])
        both = jnp.stack([chips, move(chips, flip_dp(1))], axis=1)
        both = both.reshape(TEAM * seqs * toks, 2 * HEAD)
        share = lax.dot_general(
            ordered, both, (((0,), (0,)), ((), ())), preferred_element_type=jnp.float32
        ).astype(jnp.bfloat16)
        share = share.reshape(2, 2, 4, -1, 2 * HEAD)
        kept = lax.dynamic_index_in_dim(share, z, 2, keepdims=False).astype(jnp.float32)
        for bits in range(1, 4):
            sent = lax.dynamic_index_in_dim(share, z ^ bits, 2, keepdims=False)
            kept = kept + move(sent, flip_ctx(bits)).astype(jnp.float32)

        def piece(low, high):
            value = lax.dynamic_index_in_dim(kept, y_low ^ low, 0, keepdims=False)
            return lax.dynamic_index_in_dim(value, y_high ^ high, 0, keepdims=False)

        final = piece(0, 0)
        for low, high in ((1, 0), (0, 1), (1, 1)):
            final = final + move(piece(low, high), flip_y(low, high))
        grad_parts.append(final)
    query_grad = jnp.concatenate(query_parts, axis=2)
    weight_grad = jnp.concatenate(
        [part[:, :HEAD] for part in grad_parts] + [part[:, HEAD:] for part in grad_parts], axis=1
    )
    return query_grad, weight_grad


def solution(mesh):
    in_specs = (
        P("dp", "ctx", None),
        P("dp", "ctx", None),
        P("dp", "ctx", None),
        P(),
        P("dp", None),
        P("dp", "ctx", None),
    )
    out_specs = (P("dp", "ctx", None), P(("dp", "ctx"), None))
    return jax.shard_map(
        per_device, mesh=mesh, in_specs=in_specs, out_specs=out_specs, check_vma=False
    )
```

time: 1160 us -> 486 us (0.42)
  waiting for transfers between devices: 875 us -> 148 us
  starting transfers between devices: 11.7 us -> 196 us
  matrix products: 187 us -> 9.37 us
  between operations: 20.4 us -> 48.2 us
  other arithmetic: 13.7 us -> 32.9 us
  local copies, waits for them, and re-layouts: 49.1 us -> 34.3 us
    reduce_scatter x1 -> x0, waiting for transfers between devices: 612 us -> none  [per_device(): lax.psum_scatter(lax.dot_general(piece, flat_grad, (((0,), (0,)), ((), ()...]
    ppermute x9 -> x90, starting transfers between devices: 11.1 us -> 196 us  [move(): return lax.ppermute(value, AXES, route)]
    dot_general x22 -> x5, matrix products: 187 us -> 9.37 us  [the longest x1 6.35 us: per_device(): jnp.dot(flat, kv_weight, preferred_element_type=jnp.float32)]
    unnamed x4 -> x0, waiting for transfers between devices: 82.6 us -> none
    all_gather x1 -> x0, waiting for transfers between devices: 54.7 us -> none  [per_device(): kv_whole = lax.all_gather(kv_rows, 'ctx', axis=1, tiled=True)]
    ppermute x9 -> x90, waiting for transfers between devices: 126 us -> 148 us  [move(): return lax.ppermute(value, AXES, route)]
    slice x10 -> x2, local copies, waits for them, and re-layouts: 19.4 us -> 1.53 us  [the longest x1 1.42 us: trade(): mask = jnp.arange(2, dtype=jnp.int32) == plan[step]]
  transfers between devices with their start and end apart: 12 -> 90, of which waited for: 9 -> 28; matrix products, arithmetic and copies ran while one was open for 7% -> 14% of each run, Pallas kernels for 0% -> 0%
where the time goes in v1:
time: 486 us; the launch traced here: 480 us
  starting transfers between devices  196 us (40%)
  waiting for transfers between devices  148 us (30%)
  between operations  48.2 us (10%)
  local copies, waits for them, and re-layouts  34.3 us (7%)
  other arithmetic  32.9 us (7%)
  Pallas kernels  11.3 us (2%)
  matrix products  9.37 us (2%)
    ppermute x90, starting transfers between devices, move(): return lax.ppermute(value, AXES, route)  196 us
    ppermute x90, waiting for transfers between devices, move(): return lax.ppermute(value, AXES, route)  148 us
    unnamed x69, local copies, waits for them, and re-layouts  20.9 us
    pallas_call x4, Pallas kernels, attention(): pl.pallas_call(attention_kernel, grid_spec=spec, out_shape=[jax.ShapeDtyp...  11.3 us
  transfers between devices with their start and end apart: 90, of which 28 were waited for; matrix products, arithmetic and copies ran while one was open for 14% of the time, Pallas kernels for 0%

profile of v1, /device:TPU:0, one launch (start us, length us, event | category | flops | bytes accessed | tf_op | source)
XLA Modules:
  0.0 480.2 jit_solution(7299897180029248408)
XLA Ops:
  3.4 3.6 slice_bitcast_fusion.6
  23.5 6.3 %convolution_convert_fusion = bf16[256,1024]{1,0:T(8,128)(2,1)S(1)} fusion(bf16[256,4096]{1,0:T(8,128)(2,1)} %bitcast.334, bf16[4096,1024]{1,0:T(8,128)(2,1)} %param.9), kind=kOutput, calls=%fused_computation.2 | convolution fusion | flops 2147745792 | bytes 11010048 | tf_op jit(solution)/shard_map/dot_general | solution.py:194
  110.2 5.9 %collective-permute-done.23 = bf16[256,512]{1,0:T(8,128)(2,1)S(1)} collective-permute-done((bf16[256,512]{1,0:T(8,128)(2,1)}, bf16[256,512]{1,0:T(8,128)(2,1)S(1)}, u32[]{:S(2)}, u32[]{:S(2)}) %collective-permute-start.23) | collective-permute-done | bytes 262176 | tf_op jit(solution)/shard_map/ppermute | solution.py:30
  116.1 8.0 %collective-permute-start.24 = (bf16[256,512]{1,0:T(8,128)(2,1)}, bf16[256,512]{1,0:T(8,128)(2,1)S(1)}, u32[]{:S(2)}, u32[]{:S(2)}) collective-permute-start(bf16[256,512]{1,0:T(8,128)(2,1)} %pad_maximum_fusion.17), channel_id=1, source_target_pairs={{0,40},{1,41},{2,42},{3,43},{4,44},{5,45},{6,46},{7,47},{8,32},{9,... | collective-permute-start | bytes 786440 | tf_op jit(solution)/shard_map/ppermute | solution.py:30
  128.0 5.2 %collective-permute-done.24 = bf16[256,512]{1,0:T(8,128)(2,1)S(1)} collective-permute-done((bf16[256,512]{1,0:T(8,128)(2,1)}, bf16[256,512]{1,0:T(8,128)(2,1)S(1)}, u32[]{:S(2)}, u32[]{:S(2)}) %collective-permute-start.24) | collective-permute-done | bytes 262176 | tf_op jit(solution)/shard_map/ppermute | solution.py:30
  133.2 7.4 %collective-permute-start.26 = (bf16[256,512]{1,0:T(8,128)(2,1)S(1)}, bf16[256,512]{1,0:T(8,128)(2,1)S(1)}, u32[]{:S(2)}, u32[]{:S(2)}) collective-permute-start(bf16[256,512]{1,0:T(8,128)(2,1)S(1)} %copy-done.8), channel_id=1, source_target_pairs={{0,56},{1,57},{2,58},{3,59},{4,60},{5,61},{6,62},{7,63},{8,48},{9,... | collective-permute-start | bytes 786440 | tf_op jit(solution)/shard_map/ppermute | solution.py:30
  142.3 6.8 %collective-permute-done.26 = bf16[256,512]{1,0:T(8,128)(2,1)S(1)} collective-permute-done((bf16[256,512]{1,0:T(8,128)(2,1)S(1)}, bf16[256,512]{1,0:T(8,128)(2,1)S(1)}, u32[]{:S(2)}, u32[]{:S(2)}) %collective-permute-start.26) | collective-permute-done | bytes 262176 | tf_op jit(solution)/shard_map/ppermute | solution.py:30
  173.1 44.8 %collective-permute-done.5 = bf16[128,1024]{1,0:T(8,128)(2,1)S(1)} collective-permute-done((bf16[128,1024]{1,0:T(8,128)(2,1)S(1)}, bf16[128,1024]{1,0:T(8,128)(2,1)S(1)}, u32[]{:S(2)}, u32[]{:S(2)}) %collective-permute-start.5) | collective-permute-done | bytes 262176 | tf_op jit(solution)/shard_map/ppermute | solution.py:30
  218.2 6.1 %collective-permute-start.6 = (bf16[2,128,1024]{2,1,0:T(8,128)(2,1)S(1)}, bf16[2,128,1024]{2,1,0:T(8,128)(2,1)S(1)}, u32[]{:S(2)}, u32[]{:S(2)}) collective-permute-start(bf16[2,128,1024]{2,1,0:T(8,128)(2,1)S(1)} %broadcast_select_fusion.10), channel_id=1, source_target_pairs={{0,5},{1,6},{2,7},{8,13},{9,14},{10,15},{16,21},{17,22},{18,23},{2... | collective-permute-start | bytes 1572872 | tf_op jit(solution)/shard_map/ppermute | solution.py:30
  225.6 4.2 collective-permute-start.8
  239.3 6.6 %collective-permute-done.7 = bf16[2,128,1024]{2,1,0:T(8,128)(2,1)S(1)} collective-permute-done((bf16[2,128,1024]{2,1,0:T(8,128)(2,1)S(1)}, bf16[2,128,1024]{2,1,0:T(8,128)(2,1)S(1)}, u32[]{:S(2)}, u32[]{:S(2)}) %collective-permute-start.7) | collective-permute-done | bytes 524320 | tf_op jit(solution)/shard_map/ppermute | solution.py:30
  251.2 25.1 %collective-permute-start.16 = (bf16[2,128,1024]{2,1,0:T(8,128)(2,1)S(1)}, bf16[2,128,1024]{2,1,0:T(8,128)(2,1)S(1)}, u32[]{:S(2)}, u32[]{:S(2)}) collective-permute-start(bf16[2,128,1024]{2,1,0:T(8,128)(2,1)S(1)} %dynamic-slice_bitcast_fusion.2), channel_id=1, source_target_pairs={{0,32},{1,33},{2,34},{3,35},{4,36},{5,37},{6,38},{7,39},{8,40},{9,... | collective-permute-start | bytes 1572872 | tf_op jit(solution)/shard_map/ppermute | solution.py:30
  276.3 17.5 %collective-permute-start.19 = (bf16[2,128,1024]{2,1,0:T(8,128)(2,1)S(1)}, bf16[2,128,1024]{2,1,0:T(8,128)(2,1)S(1)}, u32[]{:S(2)}, u32[]{:S(2)}) collective-permute-start(bf16[2,128,1024]{2,1,0:T(8,128)(2,1)S(1)} %dynamic-slice_bitcast_fusion), channel_id=1, source_target_pairs={{0,32},{1,33},{2,34},{3,35},{4,36},{5,37},{6,38},{7,39},{8,40},{9,... | collective-permute-start | bytes 1572872 | tf_op jit(solution)/shard_map/ppermute | solution.py:30
  294.5 14.2 %collective-permute-done.19 = bf16[2,128,1024]{2,1,0:T(8,128)(2,1)S(1)} collective-permute-done((bf16[2,128,1024]{2,1,0:T(8,128)(2,1)S(1)}, bf16[2,128,1024]{2,1,0:T(8,128)(2,1)S(1)}, u32[]{:S(2)}, u32[]{:S(2)}) %collective-permute-start.19) | collective-permute-done | bytes 524320 | tf_op jit(solution)/shard_map/ppermute | solution.py:30
  328.7 16.7 %collective-permute-done.34 = bf16[2,128,256]{2,1,0:T(8,128)(2,1)S(1)} collective-permute-done((bf16[2,128,256]{2,1,0:T(8,128)(2,1)S(1)}, bf16[2,128,256]{2,1,0:T(8,128)(2,1)S(1)}, u32[]{:S(2)}, u32[]{:S(2)}) %collective-permute-start.34) | collective-permute-done | bytes 131104 | tf_op jit(solution)/shard_map/ppermute | solution.py:30
  352.0 4.3 collective-permute-done.49
  358.9 8.4 %collective-permute-done.47 = bf16[2,128,256]{2,1,0:T(8,128)(2,1)S(1)} collective-permute-done((bf16[2,128,256]{2,1,0:T(8,128)(2,1)S(1)}, bf16[2,128,256]{2,1,0:T(8,128)(2,1)S(1)}, u32[]{:S(2)}, u32[]{:S(2)}) %collective-permute-start.47) | collective-permute-done | bytes 131104 | tf_op jit(solution)/shard_map/ppermute | solution.py:30
  375.2 3.5 collective-permute-done.62
  397.5 21.9 %collective-permute-start.67 = (bf16[2,128,256]{2,1,0:T(8,128)(2,1)S(1)}, bf16[2,128,256]{2,1,0:T(8,128)(2,1)S(1)}, u32[]{:S(2)}, u32[]{:S(2)}) collective-permute-start(bf16[2,128,256]{2,1,0:T(8,128)(2,1)S(1)} %fusion.22), channel_id=1, source_target_pairs={{0,48},{1,49},{2,50},{3,51},{4,52},{5,53},{6,54},{7,55},{8,56},{9,... | collective-permute-start | bytes 393224 | tf_op jit(solution)/shard_map/ppermute | solution.py:30
  423.9 4.9 %collective-permute-done.67 = bf16[2,128,256]{2,1,0:T(8,128)(2,1)S(1)} collective-permute-done((bf16[2,128,256]{2,1,0:T(8,128)(2,1)S(1)}, bf16[2,128,256]{2,1,0:T(8,128)(2,1)S(1)}, u32[]{:S(2)}, u32[]{:S(2)}) %collective-permute-start.67) | collective-permute-done | bytes 131104 | tf_op jit(solution)/shard_map/ppermute | solution.py:30
  431.2 5.2 %collective-permute-done.81 = bf16[2,128,256]{2,1,0:T(8,128)(2,1)S(1)} collective-permute-done((bf16[2,128,256]{2,1,0:T(8,128)(2,1)S(1)}, bf16[2,128,256]{2,1,0:T(8,128)(2,1)S(1)}, u32[]{:S(2)}, u32[]{:S(2)}) %collective-permute-start.81) | collective-permute-done | bytes 131104 | tf_op jit(solution)/shard_map/ppermute | solution.py:30
  437.6 3.4 collective-permute-start.41
  443.0 3.2 collective-permute-start.56
  449.3 3.1 collective-permute-start.71
  (340 shorter events, 195.3 us)
Async XLA Ops:
  9.5 152.6 %collective-permute-start = (bf16[2,128,1024]{2,1,0:T(8,128)(2,1)}, bf16[2,128,1024]{2,1,0:T(8,128)(2,1)}, u32[]{:S(2)}, u32[]{:S(2)}) collective-permute-start(bf16[2,128,1024]{2,1,0:T(8,128)(2,1)} %fusion.11), channel_id=1, source_target_pairs={{0,8},{1,9},{2,10},{3,11},{4,12},{5,13},{6,14},{7,15},{8,0},{9,1},... | collective-permute-start | bytes 1572872 | tf_op jit(solution)/shard_map/ppermute | solution.py:30
  10.4 151.7 %collective-permute-start.11 = (bf16[2,128,1024]{2,1,0:T(8,128)(2,1)}, bf16[2,128,1024]{2,1,0:T(8,128)(2,1)}, u32[]{:S(2)}, u32[]{:S(2)}) collective-permute-start(bf16[2,128,1024]{2,1,0:T(8,128)(2,1)} %fusion.9), channel_id=1, source_target_pairs={{0,8},{1,9},{2,10},{3,11},{4,12},{5,13},{6,14},{7,15},{8,0},{9,1},... | collective-permute-start | bytes 1572872 | tf_op jit(solution)/shard_map/ppermute | solution.py:30
  11.7 150.4 %collective-permute-start.14 = (bf16[2,128,1024]{2,1,0:T(8,128)(2,1)}, bf16[2,128,1024]{2,1,0:T(8,128)(2,1)}, u32[]{:S(2)}, u32[]{:S(2)}) collective-permute-start(bf16[2,128,1024]{2,1,0:T(8,128)(2,1)} %fusion.7), channel_id=1, source_target_pairs={{0,8},{1,9},{2,10},{3,11},{4,12},{5,13},{6,14},{7,15},{8,0},{9,1},... | collective-permute-start | bytes 1572872 | tf_op jit(solution)/shard_map/ppermute | solution.py:30
  15.3 85.3 %collective-permute-start.20 = (bf16[256,512]{1,0:T(8,128)(2,1)}, bf16[256,512]{1,0:T(8,128)(2,1)}, u32[]{:S(2)}, u32[]{:S(2)}) collective-permute-start(bf16[256,512]{1,0:T(8,128)(2,1)} %pad_maximum_fusion.13), channel_id=1, source_target_pairs={{0,8},{1,9},{2,10},{3,11},{4,12},{5,13},{6,14},{7,15},{8,0},{9,1},... | collective-permute-start | bytes 786440 | tf_op jit(solution)/shard_map/ppermute | solution.py:30
  15.7 27.7 %collective-permute-start.27 = (s32[1,3]{1,0:T(1,128)S(1)}, s32[1,3]{1,0:T(1,128)}, u32[]{:S(2)}, u32[]{:S(2)}) collective-permute-start(s32[1,3]{1,0:T(1,128)S(1)} %bitcast.363), channel_id=1, source_target_pairs={{0,8},{1,9},{2,10},{3,11},{4,12},{5,13},{6,14},{7,15},{8,0},{9,1},... | collective-permute-start | bytes 44 | tf_op jit(solution)/shard_map/ppermute | solution.py:30
  53.4 48.9 %collective-permute-start.21 = (bf16[256,512]{1,0:T(8,128)(2,1)}, bf16[256,512]{1,0:T(8,128)(2,1)}, u32[]{:S(2)}, u32[]{:S(2)}) collective-permute-start(bf16[256,512]{1,0:T(8,128)(2,1)} %pad_maximum_fusion.14), channel_id=1, source_target_pairs={{0,16},{1,17},{2,18},{3,19},{4,20},{5,21},{6,22},{7,23},{8,24},{9,... | collective-permute-start | bytes 786440 | tf_op jit(solution)/shard_map/ppermute | solution.py:30
  164.1 60.2 %collective-permute-start.1 = (bf16[2,128,1024]{2,1,0:T(8,128)(2,1)S(1)}, bf16[2,128,1024]{2,1,0:T(8,128)(2,1)S(1)}, u32[]{:S(2)}, u32[]{:S(2)}) collective-permute-start(bf16[2,128,1024]{2,1,0:T(8,128)(2,1)S(1)} %dynamic-slice_bitcast_fusion.7), channel_id=1, source_target_pairs={{0,16},{1,17},{2,18},{3,19},{4,20},{5,21},{6,22},{7,23},{8,24},{9,... | collective-permute-start | bytes 1572872 | tf_op jit(solution)/shard_map/ppermute | solution.py:30
  166.0 59.6 %collective-permute-start.12 = (bf16[2,128,1024]{2,1,0:T(8,128)(2,1)S(1)}, bf16[2,128,1024]{2,1,0:T(8,128)(2,1)S(1)}, u32[]{:S(2)}, u32[]{:S(2)}) collective-permute-start(bf16[2,128,1024]{2,1,0:T(8,128)(2,1)S(1)} %dynamic-slice_bitcast_fusion.5), channel_id=1, source_target_pairs={{0,16},{1,17},{2,18},{3,19},{4,20},{5,21},{6,22},{7,23},{8,24},{9,... | collective-permute-start | bytes 1572872 | tf_op jit(solution)/shard_map/ppermute | solution.py:30
  166.3 63.5 %collective-permute-start.15 = (bf16[2,128,1024]{2,1,0:T(8,128)(2,1)S(1)}, bf16[2,128,1024]{2,1,0:T(8,128)(2,1)S(1)}, u32[]{:S(2)}, u32[]{:S(2)}) collective-permute-start(bf16[2,128,1024]{2,1,0:T(8,128)(2,1)S(1)} %dynamic-slice_bitcast_fusion.3), channel_id=1, source_target_pairs={{0,16},{1,17},{2,18},{3,19},{4,20},{5,21},{6,22},{7,23},{8,24},{9,... | collective-permute-start | bytes 1572872 | tf_op jit(solution)/shard_map/ppermute | solution.py:30
  168.2 63.9 %collective-permute-start.18 = (bf16[2,128,1024]{2,1,0:T(8,128)(2,1)S(1)}, bf16[2,128,1024]{2,1,0:T(8,128)(2,1)S(1)}, u32[]{:S(2)}, u32[]{:S(2)}) collective-permute-start(bf16[2,128,1024]{2,1,0:T(8,128)(2,1)S(1)} %dynamic-slice_bitcast_fusion.1), channel_id=1, source_target_pairs={{0,16},{1,17},{2,18},{3,19},{4,20},{5,21},{6,22},{7,23},{8,24},{9,... | collective-permute-start | bytes 1572872 | tf_op jit(solution)/shard_map/ppermute | solution.py:30
  168.8 49.2 %collective-permute-start.5 = (bf16[128,1024]{1,0:T(8,128)(2,1)S(1)}, bf16[128,1024]{1,0:T(8,128)(2,1)S(1)}, u32[]{:S(2)}, u32[]{:S(2)}) collective-permute-start(bf16[128,1024]{1,0:T(8,128)(2,1)S(1)} %dynamic-slice_bitcast_fusion.8), channel_id=1, source_target_pairs={{0,32},{1,33},{2,34},{3,35},{4,36},{5,37},{6,38},{7,39},{8,40},{9,... | collective-permute-start | bytes 786440 | tf_op jit(solution)/shard_map/ppermute | solution.py:30
  225.6 25.7 %collective-permute-start.8 = (bf16[2,128,1024]{2,1,0:T(8,128)(2,1)S(1)}, bf16[2,128,1024]{2,1,0:T(8,128)(2,1)S(1)}, u32[]{:S(2)}, u32[]{:S(2)}) collective-permute-start(bf16[2,128,1024]{2,1,0:T(8,128)(2,1)S(1)} %broadcast_select_fusion.10), channel_id=1, source_target_pairs={{0,3},{1,4},{2,5},{3,6},{4,7},{8,11},{9,12},{10,13},{11,14},{12,15... | collective-permute-start | bytes 1572872 | tf_op jit(solution)/shard_map/ppermute | solution.py:30
  229.8 46.5 %collective-permute-start.9 = (bf16[2,128,1024]{2,1,0:T(8,128)(2,1)S(1)}, bf16[2,128,1024]{2,1,0:T(8,128)(2,1)S(1)}, u32[]{:S(2)}, u32[]{:S(2)}) collective-permute-start(bf16[2,128,1024]{2,1,0:T(8,128)(2,1)S(1)} %broadcast_select_fusion.10), channel_id=1, source_target_pairs={{0,2},{1,3},{2,4},{3,5},{4,6},{5,7},{8,10},{9,11},{10,12},{11,13},... | collective-permute-start | bytes 1572872 | tf_op jit(solution)/shard_map/ppermute | solution.py:30
  232.1 61.9 %collective-permute-start.10 = (bf16[2,128,1024]{2,1,0:T(8,128)(2,1)S(1)}, bf16[2,128,1024]{2,1,0:T(8,128)(2,1)S(1)}, u32[]{:S(2)}, u32[]{:S(2)}) collective-permute-start(bf16[2,128,1024]{2,1,0:T(8,128)(2,1)S(1)} %broadcast_select_fusion.10), channel_id=1, source_target_pairs={{0,1},{1,2},{2,3},{3,4},{4,5},{5,6},{6,7},{8,9},{9,10},{10,11},{11... | collective-permute-start | bytes 1572872 | tf_op jit(solution)/shard_map/ppermute | solution.py:30
  236.6 57.9 %collective-permute-start.2 = (bf16[2,128,1024]{2,1,0:T(8,128)(2,1)S(1)}, bf16[2,128,1024]{2,1,0:T(8,128)(2,1)S(1)}, u32[]{:S(2)}, u32[]{:S(2)}) collective-permute-start(bf16[2,128,1024]{2,1,0:T(8,128)(2,1)S(1)} %dynamic-slice_bitcast_fusion.6), channel_id=1, source_target_pairs={{0,32},{1,33},{2,34},{3,35},{4,36},{5,37},{6,38},{7,39},{8,40},{9,... | collective-permute-start | bytes 1572872 | tf_op jit(solution)/shard_map/ppermute | solution.py:30
  245.9 48.6 %collective-permute-start.13 = (bf16[2,128,1024]{2,1,0:T(8,128)(2,1)S(1)}, bf16[2,128,1024]{2,1,0:T(8,128)(2,1)S(1)}, u32[]{:S(2)}, u32[]{:S(2)}) collective-permute-start(bf16[2,128,1024]{2,1,0:T(8,128)(2,1)S(1)} %dynamic-slice_bitcast_fusion.4), channel_id=1, source_target_pairs={{0,32},{1,33},{2,34},{3,35},{4,36},{5,37},{6,38},{7,39},{8,40},{9,... | collective-permute-start | bytes 1572872 | tf_op jit(solution)/shard_map/ppermute | solution.py:30
  251.2 43.3 %collective-permute-start.16 = (bf16[2,128,1024]{2,1,0:T(8,128)(2,1)S(1)}, bf16[2,128,1024]{2,1,0:T(8,128)(2,1)S(1)}, u32[]{:S(2)}, u32[]{:S(2)}) collective-permute-start(bf16[2,128,1024]{2,1,0:T(8,128)(2,1)S(1)} %dynamic-slice_bitcast_fusion.2), channel_id=1, source_target_pairs={{0,32},{1,33},{2,34},{3,35},{4,36},{5,37},{6,38},{7,39},{8,40},{9,... | collective-permute-start | bytes 1572872 | tf_op jit(solution)/shard_map/ppermute | solution.py:30
  276.3 32.4 %collective-permute-start.19 = (bf16[2,128,1024]{2,1,0:T(8,128)(2,1)S(1)}, bf16[2,128,1024]{2,1,0:T(8,128)(2,1)S(1)}, u32[]{:S(2)}, u32[]{:S(2)}) collective-permute-start(bf16[2,128,1024]{2,1,0:T(8,128)(2,1)S(1)} %dynamic-slice_bitcast_fusion), channel_id=1, source_target_pairs={{0,32},{1,33},{2,34},{3,35},{4,36},{5,37},{6,38},{7,39},{8,40},{9,... | collective-permute-start | bytes 1572872 | tf_op jit(solution)/shard_map/ppermute | solution.py:30
  325.8 24.8 %collective-permute-start.30 = (bf16[2,128,256]{2,1,0:T(8,128)(2,1)S(1)}, bf16[2,128,256]{2,1,0:T(8,128)(2,1)S(1)}, u32[]{:S(2)}, u32[]{:S(2)}) collective-permute-start(bf16[2,128,256]{2,1,0:T(8,128)(2,1)S(1)} %get-tuple-element.63), channel_id=1, source_target_pairs={{1,0},{2,1},{3,2},{4,3},{5,4},{6,5},{7,6},{9,8},{10,9},{11,10},{12... | collective-permute-start | bytes 393224 | tf_op jit(solution)/shard_map/ppermute | solution.py:30
  388.3 31.2 %collective-permute-start.75 = (bf16[2,128,256]{2,1,0:T(8,128)(2,1)S(1)}, bf16[2,128,256]{2,1,0:T(8,128)(2,1)S(1)}, u32[]{:S(2)}, u32[]{:S(2)}) collective-permute-start(bf16[2,128,256]{2,1,0:T(8,128)(2,1)S(1)} %get-tuple-element.48), channel_id=1, source_target_pairs={{1,0},{2,1},{3,2},{4,3},{5,4},{6,5},{7,6},{9,8},{10,9},{11,10},{12... | collective-permute-start | bytes 393224 | tf_op jit(solution)/shard_map/ppermute | solution.py:30
  389.6 32.4 %collective-permute-start.52 = (bf16[2,128,256]{2,1,0:T(8,128)(2,1)S(1)}, bf16[2,128,256]{2,1,0:T(8,128)(2,1)S(1)}, u32[]{:S(2)}, u32[]{:S(2)}) collective-permute-start(bf16[2,128,256]{2,1,0:T(8,128)(2,1)S(1)} %fusion.27), channel_id=1, source_target_pairs={{0,48},{1,49},{2,50},{3,51},{4,52},{5,53},{6,54},{7,55},{8,56},{9,... | collective-permute-start | bytes 393224 | tf_op jit(solution)/shard_map/ppermute | solution.py:30
  392.2 30.5 %collective-permute-start.51 = (bf16[2,128,256]{2,1,0:T(8,128)(2,1)S(1)}, bf16[2,128,256]{2,1,0:T(8,128)(2,1)S(1)}, u32[]{:S(2)}, u32[]{:S(2)}) collective-permute-start(bf16[2,128,256]{2,1,0:T(8,128)(2,1)S(1)} %fusion.27), channel_id=1, source_target_pairs={{0,32},{1,33},{2,34},{3,35},{4,36},{5,37},{6,38},{7,39},{8,40},{9,... | collective-permute-start | bytes 393224 | tf_op jit(solution)/shard_map/ppermute | solution.py:30
  395.3 27.5 %collective-permute-start.50 = (bf16[2,128,256]{2,1,0:T(8,128)(2,1)S(1)}, bf16[2,128,256]{2,1,0:T(8,128)(2,1)S(1)}, u32[]{:S(2)}, u32[]{:S(2)}) collective-permute-start(bf16[2,128,256]{2,1,0:T(8,128)(2,1)S(1)} %fusion.27), channel_id=1, source_target_pairs={{0,16},{1,17},{2,18},{3,19},{4,20},{5,21},{6,22},{7,23},{8,24},{9,... | collective-permute-start | bytes 393224 | tf_op jit(solution)/shard_map/ppermute | solution.py:30
  397.5 31.3 %collective-permute-start.67 = (bf16[2,128,256]{2,1,0:T(8,128)(2,1)S(1)}, bf16[2,128,256]{2,1,0:T(8,128)(2,1)S(1)}, u32[]{:S(2)}, u32[]{:S(2)}) collective-permute-start(bf16[2,128,256]{2,1,0:T(8,128)(2,1)S(1)} %fusion.22), channel_id=1, source_target_pairs={{0,48},{1,49},{2,50},{3,51},{4,52},{5,53},{6,54},{7,55},{8,56},{9,... | collective-permute-start | bytes 393224 | tf_op jit(solution)/shard_map/ppermute | solution.py:30
  (84 other events, 1085.8 us)

commit v2 on v0

v2 whole, which is shorter than its diff:
```python
import functools

import jax
import jax.numpy as jnp
from jax import lax
from jax.experimental import pallas as pl
from jax.experimental.pallas import tpu as pltpu
from jax.sharding import PartitionSpec as P

HEAD = 128
ROUNDS = 3
AXES = ("dp", "ctx")
N_DP = 16
N_CTX = 8
TEAM = 8
WINDOW = 6
BLOCK = 128
GROUPS = 4
CHUNKS = 2
SHARE = GROUPS // CHUNKS
VMEM = 48 * 1024 * 1024
MASKED = -1e30
LOG2E = 1.4426950408889634
NT = (((1,), (1,)), ((), ()))
NN = (((1,), (0,)), ((), ()))
TN = (((0,), (0,)), ((), ()))


def move(value, target):
    route = []
    for dp in range(N_DP):
        for ctx in range(N_CTX):
            to_dp, to_ctx = target(dp, ctx)
            if 0 <= to_ctx < N_CTX:
                route.append((dp * N_CTX + ctx, to_dp * N_CTX + to_ctx))
    return lax.ppermute(value, AXES, route)


def flip_dp(bits):
    return lambda dp, ctx: (dp ^ bits, ctx)


def flip_ctx(bits):
    return lambda dp, ctx: (dp, ctx ^ bits)


def shift_ctx(by):
    return lambda dp, ctx: (dp, ctx + by)


def flip_y(low, high):
    return lambda dp, ctx: (dp ^ (low * 8), ctx ^ (high * 4))


ANYWHERE = pl.BlockSpec(memory_space=pl.ANY)


def light(read):
    return dict(
        compiler_params=pltpu.CompilerParams(vmem_limit_bytes=VMEM),
        cost_estimate=pl.CostEstimate(flops=0, bytes_accessed=read, transcendentals=0),
    )


def pick_kernel(step, count, plan_ref, *refs):
    came, kept = refs[:count], refs[count : 2 * count]
    send_ref, keep_ref = refs[-2:]
    same = plan_ref[step] == plan_ref[step - 1]

    def put(out, sources):
        for index, source in enumerate(sources):
            if count == 1:
                out[...] = source[...].reshape(out.shape)
            else:
                out[index] = source[...].reshape(out.shape[1:])

    @pl.when(same)
    def _():
        put(send_ref, came)
        put(keep_ref, kept)

    @pl.when(jnp.logical_not(same))
    def _():
        put(send_ref, kept)
        put(keep_ref, came)


def pick(step, plan, came, kept, chunk, chunks, held_back=()):
    toks, width = came[0].shape[-2:]
    width //= chunks
    steps = 1 if width <= 1024 else width // 1024
    block = width // steps
    first = chunk * steps
    in_specs = []
    for array in came:
        lead = array.shape[:-2]
        in_specs.append(
            pl.BlockSpec(lead + (toks, block), lambda g, p, n=len(lead): (0,) * n + (0, first + g))
        )
    for array in kept:
        if step == 1:
            in_specs.append(pl.BlockSpec((1, toks, block), lambda g, p: (1 - p[0], 0, first + g)))
        else:
            lead = array.shape[:-2]
            in_specs.append(
                pl.BlockSpec(
                    lead + (toks, block), lambda g, p, n=len(lead): (0,) * n + (0, first + g)
                )
            )
    lead = (len(came),) if len(came) > 1 else came[0].shape[:-2]
    shape = jax.ShapeDtypeStruct(lead + (toks, width), came[0].dtype)
    out = pl.BlockSpec(lead + (toks, block), lambda g, p, n=len(lead): (0,) * n + (0, g))
    return pl.pallas_call(
        functools.partial(pick_kernel, step, len(came)),
        grid_spec=pltpu.PrefetchScalarGridSpec(
            num_scalar_prefetch=1,
            grid=(steps,),
            in_specs=in_specs + [ANYWHERE] * len(held_back),
            out_specs=[out, out],
        ),
        out_shape=[shape, shape],
        **light(8 * 1024 * 1024),
    )(plan, *came, *kept, *held_back)


def rows_kernel(plan_ref, came_ref, kept_ref, *refs):
    out_ref = refs[-1]
    slot = plan_ref[ROUNDS - 1]
    out_ref[slot] = came_ref[...]
    out_ref[1 - slot] = kept_ref[...]


def rows_of(plan, came, kept, held_back=()):
    vmem = pl.BlockSpec(memory_space=pltpu.VMEM)
    return pl.pallas_call(
        rows_kernel,
        in_specs=[pl.BlockSpec(memory_space=pltpu.SMEM), vmem, vmem] + [ANYWHERE] * len(held_back),
        out_specs=vmem,
        out_shape=jax.ShapeDtypeStruct((2,) + came.shape, came.dtype),
        **light(1024 * 1024),
    )(plan, came, kept, *held_back)


def pages_kernel(count, plan_ref, *refs):
    for source, out in zip(refs[:count], refs[-count:]):
        out[...] = source[0]


def pages_of(plan, arrays, held_back=()):
    _, toks, width = arrays[0].shape
    block = min(width, 1024)
    shape = jax.ShapeDtypeStruct((toks, width), arrays[0].dtype)
    return pl.pallas_call(
        functools.partial(pages_kernel, len(arrays)),
        grid_spec=pltpu.PrefetchScalarGridSpec(
            num_scalar_prefetch=1,
            grid=(width // block,),
            in_specs=[pl.BlockSpec((1, toks, block), lambda g, p: (p[0], 0, g))] * len(arrays)
            + [ANYWHERE] * len(held_back),
            out_specs=[pl.BlockSpec((toks, block), lambda g, p: (0, g))] * len(arrays),
        ),
        out_shape=[shape] * len(arrays),
        **light(4 * 1024 * 1024),
    )(plan, *arrays, *held_back)


def sum_kernel(*refs):
    out_ref = refs[-1]
    half = out_ref.shape[-1] // 2
    for chunk in range(CHUNKS):
        parts = refs[chunk * WINDOW : (chunk + 1) * WINDOW]
        for group in range(SHARE):
            for kind in range(2):
                at = (group * 2 + kind) * HEAD
                to = kind * half + (chunk * SHARE + group) * HEAD
                total = parts[0][:, :, at : at + HEAD].astype(jnp.float32)
                for part in parts[1:]:
                    total = total + part[:, :, at : at + HEAD].astype(jnp.float32)
                out_ref[:, :, to : to + HEAD] = total.astype(out_ref.dtype)


def sum_of(chunks):
    vmem = pl.BlockSpec(memory_space=pltpu.VMEM)
    rows, toks, cols = chunks[0][0].shape
    return pl.pallas_call(
        sum_kernel,
        in_specs=[vmem] * (WINDOW * CHUNKS),
        out_specs=vmem,
        out_shape=jax.ShapeDtypeStruct((rows, toks, cols * CHUNKS), jnp.bfloat16),
        **light(4 * 1024 * 1024),
    )(*[part for parts in chunks for part in parts])


def columns_kernel(place_ref, *refs):
    sources = refs[: 2 * TEAM]
    outs = refs[-(TEAM // 2) :]
    part = sources[0].shape[1]
    for k, out in enumerate(outs):
        for side in range(2):
            for low in range(2):
                out[side, :, low * part : (low + 1) * part] = sources[(k * 2 + side) * 2 + low][...]


def columns_of(place, flat, held_back=()):
    rows, width = flat.shape
    part = width // (2 * TEAM)
    in_specs = []
    for k in range(TEAM // 2):
        for side in range(2):
            for low in range(2):
                in_specs.append(
                    pl.BlockSpec(
                        (rows, part),
                        lambda i, p, bits=2 * k + side, low=low: (0, low * TEAM + (p[0] ^ bits)),
                    )
                )
    shape = jax.ShapeDtypeStruct((2, rows, 2 * part), flat.dtype)
    out = pl.BlockSpec((2, rows, 2 * part), lambda i, p: (0, 0, 0))
    return pl.pallas_call(
        columns_kernel,
        grid_spec=pltpu.PrefetchScalarGridSpec(
            num_scalar_prefetch=1,
            grid=(1,),
            in_specs=in_specs + [ANYWHERE] * len(held_back),
            out_specs=[out] * (TEAM // 2),
        ),
        out_shape=[shape] * (TEAM // 2),
        **light(4 * 1024 * 1024),
    )(place, *([flat] * len(in_specs)), *held_back)


def attention_kernel(info_ref, *refs):
    q_ref, d_ref = refs[:2]
    k_refs = refs[2 : 2 + WINDOW]
    v_refs = refs[2 + WINDOW : 2 + 2 * WINDOW]
    start_ref = refs[2 + 2 * WINDOW]
    outs = len(refs) - 7 - WINDOW
    dq_ref = refs[outs]
    part_refs = refs[outs + 1 : outs + 1 + WINDOW]
    q_s, d_s, w_s, dp_s, acc_s, sum_s = refs[-6:]
    first = info_ref[1]
    heads = q_ref.shape[-1] // HEAD
    scale = HEAD ** (-0.5)
    for head in range(heads):
        at = slice(head * HEAD, (head + 1) * HEAD)
        q_s[head * BLOCK : (head + 1) * BLOCK, :] = q_ref[0, :, at]
        d_s[head * BLOCK : (head + 1) * BLOCK, :] = d_ref[0, :, at]
    start = start_ref[0]
    key_iota = lax.broadcasted_iota(jnp.int32, (BLOCK, BLOCK), 0)
    query_iota = lax.broadcasted_iota(jnp.int32, (BLOCK, BLOCK), 1) + (WINDOW - 1) * BLOCK
    sum_s[...] = jnp.zeros_like(sum_s)
    acc_s[...] = jnp.zeros_like(acc_s)

    for index in range(WINDOW):
        at = slice(index * BLOCK, (index + 1) * BLOCK)

        @pl.when(index >= first)
        def _():
            key_pos = key_iota + index * BLOCK
            seen = (key_pos >= start) & (key_pos <= query_iota)
            bias = jnp.concatenate([jnp.where(seen, 0.0, MASKED)] * heads, axis=1)
            scores = lax.dot_general(
                k_refs[index][0], q_s[...], NT, preferred_element_type=jnp.float32
            )
            weights = jnp.exp2(scores * (scale * LOG2E) + bias)
            dprobs = lax.dot_general(
                v_refs[index][0], d_s[...], NT, preferred_element_type=jnp.float32
            )
            w_s[at, :] = weights
            dp_s[at, :] = dprobs
            sum_s[0:1, :] += jnp.sum(weights, axis=0, keepdims=True)
            sum_s[1:2, :] += jnp.sum(weights * dprobs, axis=0, keepdims=True)

    inverse = 1.0 / sum_s[0:1, :]
    delta = sum_s[1:2, :] * inverse

    for index in range(WINDOW):
        at = slice(index * BLOCK, (index + 1) * BLOCK)

        @pl.when(index < first)
        def _():
            part_refs[index][0] = jnp.zeros(part_refs[index].shape[1:], jnp.bfloat16)

        @pl.when(index >= first)
        def _():
            probs = w_s[at, :] * inverse
            dscores = (probs * (dp_s[at, :] - delta) * scale).astype(jnp.bfloat16)
            dv = lax.dot_general(
                probs.astype(jnp.bfloat16), d_s[...], NN, preferred_element_type=jnp.float32
            )
            dk = lax.dot_general(dscores, q_s[...], NN, preferred_element_type=jnp.float32)
            part_refs[index][0, :, :HEAD] = dk.astype(jnp.bfloat16)
            part_refs[index][0, :, HEAD:] = dv.astype(jnp.bfloat16)
            acc_s[...] += lax.dot_general(
                k_refs[index][0], dscores, TN, preferred_element_type=jnp.float32
            )

    for head in range(heads):
        at = slice(head * HEAD, (head + 1) * HEAD)
        dq_ref[0, :, at] = acc_s[:, head * BLOCK : (head + 1) * BLOCK].T.astype(jnp.bfloat16)


def attention(info, page, blocks, start, chunk, dq, parts, held_back=()):
    _, toks, chunk_width = page.shape
    rows = start.shape[0]
    width = chunk_width // SHARE
    queries = width // HEAD * toks
    pairs = SHARE * queries * WINDOW * BLOCK
    in_specs = [
        pl.BlockSpec((1, toks, width), lambda g, f: (0, 0, g)),
        pl.BlockSpec((1, toks, width), lambda g, f: (1, 0, g)),
    ]
    in_specs += [pl.BlockSpec((1, BLOCK, HEAD), lambda g, f: (f[0], 0, chunk * SHARE + g))] * WINDOW
    in_specs += [
        pl.BlockSpec((1, BLOCK, HEAD), lambda g, f: (f[0], 0, GROUPS + chunk * SHARE + g))
    ] * WINDOW
    in_specs += [pl.BlockSpec((1, 1, toks), lambda g, f: (f[0], 0, 0))]
    args = [page, page] + list(blocks) + list(blocks) + [start]
    aliases = {}
    for place, array in enumerate([dq] + list(parts)):
        if array is not None:
            aliases[1 + len(args)] = place
            in_specs.append(ANYWHERE)
            args.append(array)
    in_specs += [ANYWHERE] * len(held_back)
    args += held_back
    part_shape = jax.ShapeDtypeStruct((rows, BLOCK, SHARE * 2 * HEAD), jnp.bfloat16)
    spec = pltpu.PrefetchScalarGridSpec(
        num_scalar_prefetch=1,
        grid=(SHARE,),
        in_specs=in_specs,
        out_specs=[pl.BlockSpec((1, toks, width), lambda g, f: (f[0], 0, chunk * SHARE + g))]
        + [pl.BlockSpec((1, BLOCK, 2 * HEAD), lambda g, f: (f[0], 0, g))] * WINDOW,
        scratch_shapes=[
            pltpu.VMEM((queries, HEAD), jnp.bfloat16),
            pltpu.VMEM((queries, HEAD), jnp.bfloat16),
            pltpu.VMEM((WINDOW * BLOCK, queries), jnp.float32),
            pltpu.VMEM((WINDOW * BLOCK, queries), jnp.float32),
            pltpu.VMEM((HEAD, queries), jnp.float32),
            pltpu.VMEM((8, queries), jnp.float32),
        ],
    )
    return pl.pallas_call(
        attention_kernel,
        grid_spec=spec,
        out_shape=[jax.ShapeDtypeStruct((rows, toks, GROUPS * width), jnp.bfloat16)]
        + [part_shape] * WINDOW,
        input_output_aliases=aliases,
        compiler_params=pltpu.CompilerParams(vmem_limit_bytes=VMEM),
        cost_estimate=pl.CostEstimate(
            flops=10 * pairs * HEAD, bytes_accessed=4 * 1024 * 1024, transcendentals=pairs
        ),
    )(info, *args)


def arrange_kernel(plan_ref, place_ref, *refs):
    sources, out_ref = refs[:-1], refs[-1]
    rank_me, z_me, low_me, high_me = (place_ref[i] for i in range(4))
    for rel, source in enumerate(sources):
        for page in range(2):
            rank = rank_me ^ rel
            slot = jnp.int32(page)
            for step in range(ROUNDS):
                to_rank = rank ^ (1 << step)
                goes = plan_ref[(rank ^ rank_me) * ROUNDS + step] == slot
                slot = jnp.where(goes, plan_ref[(to_rank ^ rank_me) * ROUNDS + step], slot)
                rank = jnp.where(goes, to_rank, rank)
            column = pl.multiple_of(((rank ^ rank_me) * 2 + slot) * BLOCK, BLOCK)
            data = source[page * BLOCK : (page + 1) * BLOCK, :].astype(jnp.float32)
            data = data.T.astype(jnp.bfloat16)
            for low in range(2):
                for high in range(2):
                    for z in range(4):
                        at = ((low * 2 + high) * 4 + z) * 32
                        to = (z ^ z_me) * 4 + (low ^ low_me) + (high ^ high_me) * 2
                        to = pl.multiple_of(to * 32, 32)
                        out_ref[pl.ds(to, 32), pl.ds(column, BLOCK)] = data[at : at + 32, :]


def arrange(plan_all, place, sources):
    rows, cols = sources[0].shape
    return pl.pallas_call(
        arrange_kernel,
        grid_spec=pltpu.PrefetchScalarGridSpec(
            num_scalar_prefetch=2,
            grid=(1,),
            in_specs=[pl.BlockSpec((rows, cols), lambda i, a, b: (0, 0))] * len(sources),
            out_specs=pl.BlockSpec((cols, rows * len(sources)), lambda i, a, b: (0, 0)),
        ),
        out_shape=jax.ShapeDtypeStruct((cols, rows * len(sources)), jnp.bfloat16),
        compiler_params=pltpu.CompilerParams(vmem_limit_bytes=VMEM),
        cost_estimate=pl.CostEstimate(flops=0, bytes_accessed=4 * 1024 * 1024, transcendentals=0),
    )(plan_all, place, *sources)


def product_kernel(x_ref, *refs):
    grads, outs = refs[:TEAM], refs[TEAM:]
    for z, out in enumerate(outs):
        rows = slice(z * 4 * 32, (z + 1) * 4 * 32)
        total = None
        for rel, grad in enumerate(grads):
            span = 2 * BLOCK
            block = jnp.concatenate([grad[0], grad[1]], axis=0)
            term = jnp.dot(
                x_ref[rows, rel * span : (rel + 1) * span],
                block,
                preferred_element_type=jnp.float32,
            )
            total = term if total is None else total + term
        out[...] = total.astype(out.dtype)


def product(x, grads):
    cols = grads[0].shape[-1]
    shape = (x.shape[0] // 4, cols)
    return pl.pallas_call(
        product_kernel,
        out_shape=[jax.ShapeDtypeStruct(shape, jnp.float32)]
        + [jax.ShapeDtypeStruct(shape, jnp.bfloat16)] * 3,
        compiler_params=pltpu.CompilerParams(vmem_limit_bytes=VMEM),
        cost_estimate=pl.CostEstimate(
            flops=2 * x.shape[0] * x.shape[1] * cols,
            bytes_accessed=5 * 1024 * 1024,
            transcendentals=0,
        ),
    )(x, *grads)


def per_device(tokens, queries, out_grad, kv_weight, doc_lengths, swap_plan):
    seqs, toks, width = tokens.shape
    pair = kv_weight.shape[1]
    cols = pair // 2
    group_width = queries.shape[2] // GROUPS
    dp = lax.axis_index("dp")
    ctx = lax.axis_index("ctx")
    rank = lax.rem(dp, TEAM)
    z = lax.rem(ctx, 4)
    y_high = ctx // 4
    y_low = dp // TEAM
    plan = swap_plan[0, 0]
    plans = jnp.stack([plan] + [move(plan, flip_dp(2 * k)) for k in range(1, TEAM // 2)])
    plan_all = jnp.stack([plans, move(plans, flip_dp(1))], axis=1).reshape(-1)

    ends = jnp.cumsum(doc_lengths, axis=1)
    pos = ctx * toks + jnp.arange(toks, dtype=jnp.int32)
    begun = jnp.max(
        jnp.where(ends[:, None, :] <= pos[None, :, None], ends[:, None, :], 0), axis=2
    )
    start = begun - (ctx - (WINDOW - 1)) * toks
    first = jnp.clip(start[:, 0] // BLOCK, 0, WINDOW - 1)
    start = start[:, None, :]
    row_came = plan[ROUNDS - 1]
    row_kept = 1 - row_came
    info_came = jnp.stack([row_came, jnp.where(row_came == 0, first[0], first[1])])
    info_kept = jnp.stack([row_kept, jnp.where(row_kept == 0, first[0], first[1])])

    def cross(step, value):
        return move(value, flip_dp(1 << step))

    halves = [queries, out_grad]
    flat = tokens.reshape(seqs * toks, width)
    kv = jnp.dot(flat, kv_weight, preferred_element_type=jnp.float32).astype(jnp.bfloat16)
    kv = kv.reshape(seqs, toks, pair)
    columns = columns_of(rank[None], flat)
    kv_came = cross(0, pages_of(plan, [kv], [plan_all, columns[0]])[0])
    there = {k: move(columns[k], flip_dp(2 * k)) for k in (1, 3)}
    there[0] = columns[0]
    loaded = [cross(0, one) for one in pages_of(plan, halves)]
    send, kv_kept = pick(1, plan, [kv_came], [kv], 0, 1)
    kv_came = cross(1, send)
    send, kv_kept = pick(2, plan, [kv_came], [kv_kept], 0, 1, [there[1], there[3]])
    kv_came = cross(2, send)
    send, kept = pick(1, plan, loaded, halves, 0, 1, [kv_came])
    came = cross(1, send)
    own = rows_of(plan, kv_came, kv_kept, [send])
    blocks = [move(own, shift_ctx(by)) for by in range(WINDOW - 1, 0, -1)] + [own]
    send_a, kept_a = pick(2, plan, [came], [kept], 0, CHUNKS, blocks[:4])
    came_a = cross(2, send_a)
    send_b, kept_b = pick(2, plan, [came], [kept], 1, CHUNKS, [send_a])
    came_b = cross(2, send_b)

    none = [None] * WINDOW

    def collect(parts):
        return parts[-1:] + [
            move(parts[WINDOW - 1 - by], shift_ctx(-by)) for by in range(1, WINDOW)
        ]

    dq, *parts = attention(info_kept, kept_a, blocks, start, 0, None, none)
    dq, *parts_a = attention(info_came, came_a, blocks, start, 0, dq, parts)
    dq, *parts = attention(info_kept, kept_b, blocks, start, 1, dq, none)
    parts_a = collect(parts_a)
    dq, *parts_b = attention(info_came, came_b, blocks, start, 1, dq, parts, parts_a[1:])
    late = columns_of(rank[None], flat, parts_b[:1])
    there[2] = move(late[2], flip_dp(4))
    grad = sum_of([parts_a, collect(parts_b)])

    sources = []
    for k in range(TEAM // 2):
        sources += [there[k][0], move(there[k][1], flip_dp(1))]
    place = jnp.stack([rank, z, y_low, y_high])
    arranged = arrange(plan_all, place, sources)
    grads = []
    for k in range(TEAM // 2):
        chip = move(grad, flip_dp(2 * k)) if k else grad
        grads += [chip, move(chip, flip_dp(1))]
    mine, *others = product(arranged, grads)
    for k, other in enumerate(others):
        mine = mine + move(other, flip_ctx(k + 1)).astype(jnp.float32)
    final = mine[:32]
    for k in range(1, 4):
        final = final + move(mine[32 * k : 32 * (k + 1)], flip_y(k % 2, k // 2))
    return dq, final


def solution(mesh):
    in_specs = (
        P("dp", "ctx", None),
        P("dp", "ctx", None),
        P("dp", "ctx", None),
        P(),
        P("dp", None),
        P("dp", "ctx", None),
    )
    out_specs = (P("dp", "ctx", None), P(("dp", "ctx"), None))
    return jax.shard_map(
        per_device, mesh=mesh, in_specs=in_specs, out_specs=out_specs, check_vma=False
    )
```

time: 1160 us -> 280 us (0.24)
  waiting for transfers between devices: 875 us -> 130 us
  matrix products: 187 us -> 6.58 us
  starting transfers between devices: 11.7 us -> 76.9 us
  Pallas kernels: 0 us -> 46.6 us
  local copies, waits for them, and re-layouts: 49.1 us -> 11.1 us
  between operations: 20.4 us -> 4.9 us
  other arithmetic: 13.7 us -> 2 us
    reduce_scatter x1 -> x0, waiting for transfers between devices: 612 us -> none  [per_device(): lax.psum_scatter(lax.dot_general(piece, flat_grad, (((0,), (0,)), ((), ()...]
    dot_general x22 -> x1, matrix products: 187 us -> 6.58 us  [per_device(): jnp.dot(flat, kv_weight, preferred_element_type=jnp.float32)]
    unnamed x4 -> x0, waiting for transfers between devices: 82.6 us -> none
    ppermute x9 -> x47, starting transfers between devices: 11.1 us -> 76.9 us  [move(): return lax.ppermute(value, AXES, route)]
    all_gather x1 -> x0, waiting for transfers between devices: 54.7 us -> none  [per_device(): kv_whole = lax.all_gather(kv_rows, 'ctx', axis=1, tiled=True)]
    pallas_call x0 -> x17, Pallas kernels: none -> 46.6 us  [the longest x4 18.6 us: attention(): pl.pallas_call(attention_kernel, grid_spec=spec, out_shape=[jax.ShapeDtyp...]
    slice x10 -> x4, local copies, waits for them, and re-layouts: 19.4 us -> 1.37 us  [the longest x1 0.65 us: per_device(): first[1]]
    ppermute x9 -> x47, waiting for transfers between devices: 126 us -> 130 us  [move(): return lax.ppermute(value, AXES, route)]
  transfers between devices with their start and end apart: 12 -> 47, of which waited for: 9 -> 26; matrix products, arithmetic and copies ran while one was open for 7% -> 3% of each run, Pallas kernels for 0% -> 10%
where the time goes in v2:
time: 280 us; the launch traced here: 278 us
  waiting for transfers between devices  130 us (46%)
  starting transfers between devices  76.9 us (27%)
  Pallas kernels  46.6 us (17%)
  local copies, waits for them, and re-layouts  11.1 us (4%)
  matrix products  6.58 us (2%)
  between operations  4.9 us (2%)
    ppermute x47, waiting for transfers between devices, move(): return lax.ppermute(value, AXES, route)  130 us
    ppermute x47, starting transfers between devices, move(): return lax.ppermute(value, AXES, route)  76.9 us
    pallas_call x4, Pallas kernels, attention(): pl.pallas_call(attention_kernel, grid_spec=spec, out_shape=[jax.ShapeDtyp...  18.6 us
    pallas_call x5, Pallas kernels, pick(): pl.pallas_call(functools.partial(pick_kernel, step, len(came)), grid_spec...  12.5 us
    unnamed x36, local copies, waits for them, and re-layouts  9.45 us
    dot_general x1, matrix products, per_device(): jnp.dot(flat, kv_weight, preferred_element_type=jnp.float32)  6.58 us
  transfers between devices with their start and end apart: 47, of which 26 were waited for; matrix products, arithmetic and copies ran while one was open for 3% of the time, Pallas kernels for 10%

profile of v2, /device:TPU:0, one launch (start us, length us, event | category | flops | bytes accessed | tf_op | source)
XLA Modules:
  0.0 277.8 jit_solution(2232762200036903594)
XLA Ops:
  11.8 6.6 %convolution_convert_fusion = bf16[256,1024]{1,0:T(8,128)(2,1)} fusion(bf16[256,4096]{1,0:T(8,128)(2,1)S(1)} %bitcast.41, bf16[4096,1024]{1,0:T(8,128)(2,1)} %param.9), kind=kOutput, calls=%fused_computation | convolution fusion | flops 2147745792 | bytes 11010048 | tf_op jit(solution)/shard_map/dot_general | solution.py:462
  28.7 6.8 %collective-permute-done.8.refs_2_ = bf16[2,256,512]{2,1,0:T(8,128)(2,1)S(1)} collective-permute-done((bf16[2,256,512]{2,1,0:T(8,128)(2,1)}, bf16[2,256,512]{2,1,0:T(8,128)(2,1)S(1)}, u32[]{:S(2)}, u32[]{:S(2)}) %collective-permute-start.8) | collective-permute-done | bytes 524320 | tf_op jit(solution)/shard_map/ppermute | solution.py:36
  35.5 5.4 %collective-permute-done.9.refs_3_ = bf16[2,256,512]{2,1,0:T(8,128)(2,1)S(1)} collective-permute-done((bf16[2,256,512]{2,1,0:T(8,128)(2,1)}, bf16[2,256,512]{2,1,0:T(8,128)(2,1)S(1)}, u32[]{:S(2)}, u32[]{:S(2)}) %collective-permute-start.9) | collective-permute-done | bytes 524320 | tf_op jit(solution)/shard_map/ppermute | solution.py:36
  44.7 6.9 %collective-permute-done.10.refs_4_.came_ref = bf16[128,1024]{1,0:T(8,128)(2,1)S(1)} collective-permute-done((bf16[128,1024]{1,0:T(8,128)(2,1)S(1)}, bf16[128,1024]{1,0:T(8,128)(2,1)S(1)}, u32[]{:S(2)}, u32[]{:S(2)}) %collective-permute-start.10) | collective-permute-done | bytes 262176 | tf_op jit(solution)/shard_map/ppermute | solution.py:36
  51.6 5.3 %shard_map.82 = (bf16[2,128,4096]{2,1,0:T(8,128)(2,1)}, bf16[2,128,4096]{2,1,0:T(8,128)(2,1)}) custom-call(s32[3]{0:T(128)S(1)} %bitcast.84, bf16[128,4096]{1,0:T(8,128)(2,1)} %collective-permute-done.refs_0_, bf16[128,4096]{1,0:T(8,128)(2,1)} %collective-permute-done.1.refs_1_, bf16[2,128,4096]{2,1,0:T(8,128)(2,1)} %refs_2_.1, ...), custom_call_target="tpu_custom_call" | custom-call | bytes 8388608 | tf_op jit(solution)/shard_map/pallas_call | solution.py:113
  58.8 5.8 %collective-permute-start.15 = (bf16[2,128,1024]{2,1,0:T(8,128)(2,1)}, bf16[2,128,1024]{2,1,0:T(8,128)(2,1)S(1)}, u32[]{:S(2)}, u32[]{:S(2)}) collective-permute-start(bf16[2,128,1024]{2,1,0:T(8,128)(2,1)} %shard_map.83.refs_7_.refs_13_), channel_id=1, source_target_pairs={{0,2},{1,3},{2,4},{3,5},{4,6},{5,7},{8,10},{9,11},{10,12},{11,13},... | collective-permute-start | bytes 1572872 | tf_op jit(solution)/shard_map/ppermute | solution.py:36
  64.6 5.3 %collective-permute-start.14 = (bf16[2,128,1024]{2,1,0:T(8,128)(2,1)}, bf16[2,128,1024]{2,1,0:T(8,128)(2,1)S(1)}, u32[]{:S(2)}, u32[]{:S(2)}) collective-permute-start(bf16[2,128,1024]{2,1,0:T(8,128)(2,1)} %shard_map.83.refs_7_.refs_13_), channel_id=1, source_target_pairs={{0,3},{1,4},{2,5},{3,6},{4,7},{8,11},{9,12},{10,13},{11,14},{12,15... | collective-permute-start | bytes 1572872 | tf_op jit(solution)/shard_map/ppermute | solution.py:36
  76.7 9.4 %collective-permute-done.14.refs_4_.refs_10_ = bf16[2,128,1024]{2,1,0:T(8,128)(2,1)S(1)} collective-permute-done((bf16[2,128,1024]{2,1,0:T(8,128)(2,1)}, bf16[2,128,1024]{2,1,0:T(8,128)(2,1)S(1)}, u32[]{:S(2)}, u32[]{:S(2)}) %collective-permute-start.14) | collective-permute-done | bytes 524320 | tf_op jit(solution)/shard_map/ppermute | solution.py:36
  86.1 6.3 %collective-permute-done.12.refs_2_.refs_8_ = bf16[2,128,1024]{2,1,0:T(8,128)(2,1)} collective-permute-done((bf16[2,128,1024]{2,1,0:T(8,128)(2,1)}, bf16[2,128,1024]{2,1,0:T(8,128)(2,1)}, u32[]{:S(2)}, u32[]{:S(2)}) %collective-permute-start.12) | collective-permute-done | bytes 524320 | tf_op jit(solution)/shard_map/ppermute | solution.py:36
  92.4 11.0 %collective-permute-done.11.refs_0_ = bf16[2,128,4096]{2,1,0:T(8,128)(2,1)} collective-permute-done((bf16[2,128,4096]{2,1,0:T(8,128)(2,1)}, bf16[2,128,4096]{2,1,0:T(8,128)(2,1)}, u32[]{:S(2)}, u32[]{:S(2)}) %collective-permute-start.11) | collective-permute-done | bytes 2097184 | tf_op jit(solution)/shard_map/ppermute | solution.py:36
  115.0 4.6 %collective-permute-start.17 = (bf16[2,128,1024]{2,1,0:T(8,128)(2,1)}, bf16[2,128,1024]{2,1,0:T(8,128)(2,1)}, u32[]{:S(2)}, u32[]{:S(2)}) collective-permute-start(bf16[2,128,1024]{2,1,0:T(8,128)(2,1)} %shard_map.83.refs_7_.refs_13_), channel_id=1, source_target_pairs={{0,1},{1,2},{2,3},{3,4},{4,5},{5,6},{6,7},{8,9},{9,10},{10,11},{11... | collective-permute-start | bytes 1572872 | tf_op jit(solution)/shard_map/ppermute | solution.py:36
  135.3 4.7 %shard_map.87 = (bf16[2,128,4096]{2,1,0:T(8,128)(2,1)}, bf16[2,128,512]{2,1,0:T(8,128)(2,1)S(1)}, bf16[2,128,512]{2,1,0:T(8,128)(2,1)S(1)}, bf16[2,128,512]{2,1,...) custom-call(s32[2]{0:T(128)S(1)} %pad_add_fusion.2.info_ref, ...), custom_call_target="tpu_custom_call", output_to_operand_aliasing={{0}: (16, {}), {1}: (17, {}), {2}: (18, {}), {3}: (19, {}),... | custom-call | flops 2013265920 | bytes 4194304 | tf_op jit(solution)/shard_map/pallas_call | solution.py:343
  145.2 9.2 %collective-permute-done.16.refs_0_.refs_1_ = bf16[2,128,2048]{2,1,0:T(8,128)(2,1)} collective-permute-done((bf16[2,128,2048]{2,1,0:T(8,128)(2,1)}, bf16[2,128,2048]{2,1,0:T(8,128)(2,1)}, u32[]{:S(2)}, u32[]{:S(2)}) %collective-permute-start.16) | collective-permute-done | bytes 1048608 | tf_op jit(solution)/shard_map/ppermute | solution.py:36
  155.9 4.6 %shard_map.88 = (bf16[2,128,4096]{2,1,0:T(8,128)(2,1)}, bf16[2,128,512]{2,1,0:T(8,128)(2,1)S(1)}, bf16[2,128,512]{2,1,0:T(8,128)(2,1)S(1)}, bf16[2,128,512]{2,1,...) custom-call(s32[2]{0:T(128)S(1)} %pad_add_fusion.3.info_ref, ...), custom_call_target="tpu_custom_call", output_to_operand_aliasing={{0}: (16, {})} | custom-call | flops 2013265920 | bytes 4194304 | tf_op jit(solution)/shard_map/pallas_call | solution.py:343
  161.8 11.1 %collective-permute-done.22.refs_25_.refs_4_ = bf16[2,128,512]{2,1,0:T(8,128)(2,1)S(1)} collective-permute-done((bf16[2,128,512]{2,1,0:T(8,128)(2,1)S(1)}, bf16[2,128,512]{2,1,0:T(8,128)(2,1)S(1)}, u32[]{:S(2)}, u32[]{:S(2)}) %collective-permute-start.22) | collective-permute-done | bytes 262176 | tf_op jit(solution)/shard_map/ppermute | solution.py:36
  176.5 4.7 %shard_map.89 = (bf16[2,128,4096]{2,1,0:T(8,128)(2,1)}, bf16[2,128,512]{2,1,0:T(8,128)(2,1)S(1)}, bf16[2,128,512]{2,1,0:T(8,128)(2,1)S(1)}, bf16[2,128,512]{2,1,...) custom-call(s32[2]{0:T(128)S(1)} %pad_add_fusion.2.info_ref, ...), custom_call_target="tpu_custom_call", output_to_operand_aliasing={{0}: (16, {}), {1}: (17, {}), {2}: (18, {}), {3}: (19, {}),... | custom-call | flops 2013265920 | bytes 4194304 | tf_op jit(solution)/shard_map/pallas_call | solution.py:343
  190.6 5.7 %collective-permute-done.30.refs_8_ = bf16[2,128,512]{2,1,0:T(8,128)(2,1)S(1)} collective-permute-done((bf16[2,128,512]{2,1,0:T(8,128)(2,1)S(1)}, bf16[2,128,512]{2,1,0:T(8,128)(2,1)S(1)}, u32[]{:S(2)}, u32[]{:S(2)}) %collective-permute-start.30) | collective-permute-done | bytes 262176 | tf_op jit(solution)/shard_map/ppermute | solution.py:36
  196.2 5.8 %collective-permute-start.26 = (bf16[2,256,512]{2,1,0:T(8,128)(2,1)S(1)}, bf16[2,256,512]{2,1,0:T(8,128)(2,1)S(1)}, u32[]{:S(2)}, u32[]{:S(2)}) collective-permute-start(bf16[2,256,512]{2,1,0:T(8,128)(2,1)S(1)} %get-tuple-element.87), channel_id=1, source_target_pairs={{0,32},{1,33},{2,34},{3,35},{4,36},{5,37},{6,38},{7,39},{8,40},{9,... | collective-permute-start | bytes 1572872 | tf_op jit(solution)/shard_map/ppermute | solution.py:36
  202.0 4.8 %collective-permute-done.32.refs_10_ = bf16[2,128,512]{2,1,0:T(8,128)(2,1)S(1)} collective-permute-done((bf16[2,128,512]{2,1,0:T(8,128)(2,1)S(1)}, bf16[2,128,512]{2,1,0:T(8,128)(2,1)S(1)}, u32[]{:S(2)}, u32[]{:S(2)}) %collective-permute-start.32) | collective-permute-done | bytes 262176 | tf_op jit(solution)/shard_map/ppermute | solution.py:36
  208.7 5.3 %collective-permute-start.39 = (bf16[2,128,1024]{2,1,0:T(8,128)(2,1)S(1)}, bf16[2,128,1024]{2,1,0:T(8,128)(2,1)S(1)}, u32[]{:S(2)}, u32[]{:S(2)}) collective-permute-start(bf16[2,128,1024]{2,1,0:T(8,128)(2,1)S(1)} %shard_map.92.refs_0_), channel_id=1, source_target_pairs={{0,48},{1,49},{2,50},{3,51},{4,52},{5,53},{6,54},{7,55},{8,56},{9,... | collective-permute-start | bytes 1572872 | tf_op jit(solution)/shard_map/ppermute | solution.py:36
  219.3 14.6 %collective-permute-done.39.refs_6_ = bf16[2,128,1024]{2,1,0:T(8,128)(2,1)S(1)} collective-permute-done((bf16[2,128,1024]{2,1,0:T(8,128)(2,1)S(1)}, bf16[2,128,1024]{2,1,0:T(8,128)(2,1)S(1)}, u32[]{:S(2)}, u32[]{:S(2)}) %collective-permute-start.39) | collective-permute-done | bytes 524320 | tf_op jit(solution)/shard_map/ppermute | solution.py:36
  242.2 4.8 %shard_map.93 = (f32[128,1024]{1,0:T(8,128)S(1)}, bf16[128,1024]{1,0:T(8,128)(2,1)S(1)}, bf16[128,1024]{1,0:T(8,128)(2,1)S(1)}, bf16[128,1024]{1,0:T(8,128)(2,1)S(1)}) custom-call(bf16[512,2048]{1,0:T(8,128)(2,1)} %copy-done.6, bf16[2,128,1024]{2,1,0:T(8,128)(2,1)S(1)} %shard_map.92.refs_0_, bf16[2,128,1024]{2,1,0:T(8,128)(2,1)} %collective-permute-done.34.refs_1_, ...), custom_call_target="tpu_custom_call" | custom-call | flops 2147483648 | bytes 5242880 | tf_op jit(solution)/shard_map/pallas_call | solution.py:416
  256.3 4.7 %collective-permute-done.42 = bf16[128,1024]{1,0:T(8,128)(2,1)S(1)} collective-permute-done((bf16[128,1024]{1,0:T(8,128)(2,1)S(1)}, bf16[128,1024]{1,0:T(8,128)(2,1)S(1)}, u32[]{:S(2)}, u32[]{:S(2)}) %collective-permute-start.42) | collective-permute-done | bytes 262176 | tf_op jit(solution)/shard_map/ppermute | solution.py:36
  263.8 4.9 %collective-permute-start.44 = (f32[32,1024]{1,0:T(8,128)S(1)}, f32[32,1024]{1,0:T(8,128)S(1)}, u32[]{:S(2)}, u32[]{:S(2)}) collective-permute-start(f32[32,1024]{1,0:T(8,128)S(1)} %get-tuple-element.98), channel_id=1, source_target_pairs={{0,64},{1,65},{2,66},{3,67},{4,68},{5,69},{6,70},{7,71},{8,72},{9,... | collective-permute-start | bytes 393224 | tf_op jit(solution)/shard_map/ppermute | solution.py:36
  (146 shorter events, 114.4 us)
Async XLA Ops:
  0.6 19.9 %collective-permute-start.4 = (s32[3]{0:T(128)}, s32[3]{0:T(128)S(1)}, u32[]{:S(2)}, u32[]{:S(2)}) collective-permute-start(s32[3]{0:T(128)} %bitcast.76), channel_id=1, source_target_pairs={{0,48},{1,49},{2,50},{3,51},{4,52},{5,53},{6,54},{7,55},{8,56},{9,... | collective-permute-start | bytes 44 | tf_op jit(solution)/shard_map/ppermute | solution.py:36
  3.6 18.5 %collective-permute-start.3 = (s32[3]{0:T(128)}, s32[3]{0:T(128)S(1)}, u32[]{:S(2)}, u32[]{:S(2)}) collective-permute-start(s32[3]{0:T(128)} %bitcast.77), channel_id=1, source_target_pairs={{0,32},{1,33},{2,34},{3,35},{4,36},{5,37},{6,38},{7,39},{8,40},{9,... | collective-permute-start | bytes 44 | tf_op jit(solution)/shard_map/ppermute | solution.py:36
  11.3 40.3 %collective-permute-start = (bf16[128,4096]{1,0:T(8,128)(2,1)}, bf16[128,4096]{1,0:T(8,128)(2,1)}, u32[]{:S(2)}, u32[]{:S(2)}) collective-permute-start(bf16[128,4096]{1,0:T(8,128)(2,1)} %get-tuple-element.50), channel_id=1, source_target_pairs={{0,8},{1,9},{2,10},{3,11},{4,12},{5,13},{6,14},{7,15},{8,0},{9,1},... | collective-permute-start | bytes 3145736 | tf_op jit(solution)/shard_map/ppermute | solution.py:36
  11.3 40.3 %collective-permute-start.1 = (bf16[128,4096]{1,0:T(8,128)(2,1)}, bf16[128,4096]{1,0:T(8,128)(2,1)}, u32[]{:S(2)}, u32[]{:S(2)}) collective-permute-start(bf16[128,4096]{1,0:T(8,128)(2,1)} %get-tuple-element.51), channel_id=1, source_target_pairs={{0,8},{1,9},{2,10},{3,11},{4,12},{5,13},{6,14},{7,15},{8,0},{9,1},... | collective-permute-start | bytes 3145736 | tf_op jit(solution)/shard_map/ppermute | solution.py:36
  56.9 46.5 %collective-permute-start.11 = (bf16[2,128,4096]{2,1,0:T(8,128)(2,1)}, bf16[2,128,4096]{2,1,0:T(8,128)(2,1)}, u32[]{:S(2)}, u32[]{:S(2)}) collective-permute-start(bf16[2,128,4096]{2,1,0:T(8,128)(2,1)} %get-tuple-element.58.refs_0_), channel_id=1, source_target_pairs={{0,16},{1,17},{2,18},{3,19},{4,20},{5,21},{6,22},{7,23},{8,24},{9,... | collective-permute-start | bytes 6291464 | tf_op jit(solution)/shard_map/ppermute | solution.py:36
  64.6 21.5 %collective-permute-start.14 = (bf16[2,128,1024]{2,1,0:T(8,128)(2,1)}, bf16[2,128,1024]{2,1,0:T(8,128)(2,1)S(1)}, u32[]{:S(2)}, u32[]{:S(2)}) collective-permute-start(bf16[2,128,1024]{2,1,0:T(8,128)(2,1)} %shard_map.83.refs_7_.refs_13_), channel_id=1, source_target_pairs={{0,3},{1,4},{2,5},{3,6},{4,7},{8,11},{9,12},{10,13},{11,14},{12,15... | collective-permute-start | bytes 1572872 | tf_op jit(solution)/shard_map/ppermute | solution.py:36
  72.4 20.0 %collective-permute-start.12 = (bf16[2,128,1024]{2,1,0:T(8,128)(2,1)}, bf16[2,128,1024]{2,1,0:T(8,128)(2,1)}, u32[]{:S(2)}, u32[]{:S(2)}) collective-permute-start(bf16[2,128,1024]{2,1,0:T(8,128)(2,1)} %shard_map.83.refs_7_.refs_13_), channel_id=1, source_target_pairs={{0,5},{1,6},{2,7},{8,13},{9,14},{10,15},{16,21},{17,22},{18,23},{2... | collective-permute-start | bytes 1572872 | tf_op jit(solution)/shard_map/ppermute | solution.py:36
  107.4 27.9 %collective-permute-start.18 = (bf16[2,128,2048]{2,1,0:T(8,128)(2,1)}, bf16[2,128,2048]{2,1,0:T(8,128)(2,1)}, u32[]{:S(2)}, u32[]{:S(2)}) collective-permute-start(bf16[2,128,2048]{2,1,0:T(8,128)(2,1)} %get-tuple-element.61.refs_2_), channel_id=1, source_target_pairs={{0,32},{1,33},{2,34},{3,35},{4,36},{5,37},{6,38},{7,39},{8,40},{9,... | collective-permute-start | bytes 3145736 | tf_op jit(solution)/shard_map/ppermute | solution.py:36
  113.2 41.2 %collective-permute-start.16 = (bf16[2,128,2048]{2,1,0:T(8,128)(2,1)}, bf16[2,128,2048]{2,1,0:T(8,128)(2,1)}, u32[]{:S(2)}, u32[]{:S(2)}) collective-permute-start(bf16[2,128,2048]{2,1,0:T(8,128)(2,1)} %get-tuple-element.62), channel_id=1, source_target_pairs={{0,32},{1,33},{2,34},{3,35},{4,36},{5,37},{6,38},{7,39},{8,40},{9,... | collective-permute-start | bytes 3145736 | tf_op jit(solution)/shard_map/ppermute | solution.py:36
  140.0 20.5 %collective-permute-start.19 = (bf16[2,128,512]{2,1,0:T(8,128)(2,1)S(1)}, bf16[2,128,512]{2,1,0:T(8,128)(2,1)S(1)}, u32[]{:S(2)}, u32[]{:S(2)}) collective-permute-start(bf16[2,128,512]{2,1,0:T(8,128)(2,1)S(1)} %get-tuple-element.80), channel_id=1, source_target_pairs={{1,0},{2,1},{3,2},{4,3},{5,4},{6,5},{7,6},{9,8},{10,9},{11,10},{12... | collective-permute-start | bytes 786440 | tf_op jit(solution)/shard_map/ppermute | solution.py:36
  141.3 19.3 %collective-permute-start.20 = (bf16[2,128,512]{2,1,0:T(8,128)(2,1)S(1)}, bf16[2,128,512]{2,1,0:T(8,128)(2,1)S(1)}, u32[]{:S(2)}, u32[]{:S(2)}) collective-permute-start(bf16[2,128,512]{2,1,0:T(8,128)(2,1)S(1)} %get-tuple-element.81), channel_id=1, source_target_pairs={{2,0},{3,1},{4,2},{5,3},{6,4},{7,5},{10,8},{11,9},{12,10},{13,11},... | collective-permute-start | bytes 786440 | tf_op jit(solution)/shard_map/ppermute | solution.py:36
  142.6 19.2 %collective-permute-start.21 = (bf16[2,128,512]{2,1,0:T(8,128)(2,1)S(1)}, bf16[2,128,512]{2,1,0:T(8,128)(2,1)S(1)}, u32[]{:S(2)}, u32[]{:S(2)}) collective-permute-start(bf16[2,128,512]{2,1,0:T(8,128)(2,1)S(1)} %get-tuple-element.82), channel_id=1, source_target_pairs={{3,0},{4,1},{5,2},{6,3},{7,4},{11,8},{12,9},{13,10},{14,11},{15,12... | collective-permute-start | bytes 786440 | tf_op jit(solution)/shard_map/ppermute | solution.py:36
  143.9 29.0 %collective-permute-start.22 = (bf16[2,128,512]{2,1,0:T(8,128)(2,1)S(1)}, bf16[2,128,512]{2,1,0:T(8,128)(2,1)S(1)}, u32[]{:S(2)}, u32[]{:S(2)}) collective-permute-start(bf16[2,128,512]{2,1,0:T(8,128)(2,1)S(1)} %get-tuple-element.83), channel_id=1, source_target_pairs={{4,0},{5,1},{6,2},{7,3},{12,8},{13,9},{14,10},{15,11},{20,16},{21,... | collective-permute-start | bytes 786440 | tf_op jit(solution)/shard_map/ppermute | solution.py:36
  154.4 22.1 %collective-permute-start.23 = (bf16[2,128,512]{2,1,0:T(8,128)(2,1)S(1)}, bf16[2,128,512]{2,1,0:T(8,128)(2,1)S(1)}, u32[]{:S(2)}, u32[]{:S(2)}) collective-permute-start(bf16[2,128,512]{2,1,0:T(8,128)(2,1)S(1)} %get-tuple-element.84), channel_id=1, source_target_pairs={{5,0},{6,1},{7,2},{13,8},{14,9},{15,10},{21,16},{22,17},{23,18},{2... | collective-permute-start | bytes 786440 | tf_op jit(solution)/shard_map/ppermute | solution.py:36
  183.8 18.2 %collective-permute-start.31 = (bf16[2,128,512]{2,1,0:T(8,128)(2,1)S(1)}, bf16[2,128,512]{2,1,0:T(8,128)(2,1)S(1)}, u32[]{:S(2)}, u32[]{:S(2)}) collective-permute-start(bf16[2,128,512]{2,1,0:T(8,128)(2,1)S(1)} %get-tuple-element.92), channel_id=1, source_target_pairs={{3,0},{4,1},{5,2},{6,3},{7,4},{11,8},{12,9},{13,10},{14,11},{15,12... | collective-permute-start | bytes 786440 | tf_op jit(solution)/shard_map/ppermute | solution.py:36
  185.1 21.7 %collective-permute-start.32 = (bf16[2,128,512]{2,1,0:T(8,128)(2,1)S(1)}, bf16[2,128,512]{2,1,0:T(8,128)(2,1)S(1)}, u32[]{:S(2)}, u32[]{:S(2)}) collective-permute-start(bf16[2,128,512]{2,1,0:T(8,128)(2,1)S(1)} %get-tuple-element.93), channel_id=1, source_target_pairs={{4,0},{5,1},{6,2},{7,3},{12,8},{13,9},{14,10},{15,11},{20,16},{21,... | collective-permute-start | bytes 786440 | tf_op jit(solution)/shard_map/ppermute | solution.py:36
  186.4 21.9 %collective-permute-start.33 = (bf16[2,128,512]{2,1,0:T(8,128)(2,1)S(1)}, bf16[2,128,512]{2,1,0:T(8,128)(2,1)S(1)}, u32[]{:S(2)}, u32[]{:S(2)}) collective-permute-start(bf16[2,128,512]{2,1,0:T(8,128)(2,1)S(1)} %get-tuple-element.86.refs_16_), channel_id=1, source_target_pairs={{5,0},{6,1},{7,2},{13,8},{14,9},{15,10},{21,16},{22,17},{23,18},{2... | collective-permute-start | bytes 786440 | tf_op jit(solution)/shard_map/ppermute | solution.py:36
  190.6 26.6 %collective-permute-start.24 = (bf16[256,512]{1,0:T(8,128)(2,1)S(1)}, bf16[256,512]{1,0:T(8,128)(2,1)S(1)}, u32[]{:S(2)}, u32[]{:S(2)}) collective-permute-start(bf16[256,512]{1,0:T(8,128)(2,1)S(1)} %get-tuple-element.107), channel_id=1, source_target_pairs={{0,8},{1,9},{2,10},{3,11},{4,12},{5,13},{6,14},{7,15},{8,0},{9,1},... | collective-permute-start | bytes 786440 | tf_op jit(solution)/shard_map/ppermute | solution.py:36
  196.2 22.7 %collective-permute-start.26 = (bf16[2,256,512]{2,1,0:T(8,128)(2,1)S(1)}, bf16[2,256,512]{2,1,0:T(8,128)(2,1)S(1)}, u32[]{:S(2)}, u32[]{:S(2)}) collective-permute-start(bf16[2,256,512]{2,1,0:T(8,128)(2,1)S(1)} %get-tuple-element.87), channel_id=1, source_target_pairs={{0,32},{1,33},{2,34},{3,35},{4,36},{5,37},{6,38},{7,39},{8,40},{9,... | collective-permute-start | bytes 1572872 | tf_op jit(solution)/shard_map/ppermute | solution.py:36
  208.7 25.2 %collective-permute-start.39 = (bf16[2,128,1024]{2,1,0:T(8,128)(2,1)S(1)}, bf16[2,128,1024]{2,1,0:T(8,128)(2,1)S(1)}, u32[]{:S(2)}, u32[]{:S(2)}) collective-permute-start(bf16[2,128,1024]{2,1,0:T(8,128)(2,1)S(1)} %shard_map.92.refs_0_), channel_id=1, source_target_pairs={{0,48},{1,49},{2,50},{3,51},{4,52},{5,53},{6,54},{7,55},{8,56},{9,... | collective-permute-start | bytes 1572872 | tf_op jit(solution)/shard_map/ppermute | solution.py:36
  214.1 19.9 %collective-permute-start.37 = (bf16[2,128,1024]{2,1,0:T(8,128)(2,1)S(1)}, bf16[2,128,1024]{2,1,0:T(8,128)(2,1)}, u32[]{:S(2)}, u32[]{:S(2)}) collective-permute-start(bf16[2,128,1024]{2,1,0:T(8,128)(2,1)S(1)} %shard_map.92.refs_0_), channel_id=1, source_target_pairs={{0,32},{1,33},{2,34},{3,35},{4,36},{5,37},{6,38},{7,39},{8,40},{9,... | collective-permute-start | bytes 1572872 | tf_op jit(solution)/shard_map/ppermute | solution.py:36
  217.1 20.1 %collective-permute-start.35 = (bf16[2,128,1024]{2,1,0:T(8,128)(2,1)S(1)}, bf16[2,128,1024]{2,1,0:T(8,128)(2,1)}, u32[]{:S(2)}, u32[]{:S(2)}) collective-permute-start(bf16[2,128,1024]{2,1,0:T(8,128)(2,1)S(1)} %shard_map.92.refs_0_), channel_id=1, source_target_pairs={{0,16},{1,17},{2,18},{3,19},{4,20},{5,21},{6,22},{7,23},{8,24},{9,... | collective-permute-start | bytes 1572872 | tf_op jit(solution)/shard_map/ppermute | solution.py:36
  218.7 18.5 %collective-permute-start.28 = (bf16[256,512]{1,0:T(8,128)(2,1)S(1)}, bf16[256,512]{1,0:T(8,128)(2,1)S(1)}, u32[]{:S(2)}, u32[]{:S(2)}) collective-permute-start(bf16[256,512]{1,0:T(8,128)(2,1)S(1)} %get-tuple-element.101), channel_id=1, source_target_pairs={{0,8},{1,9},{2,10},{3,11},{4,12},{5,13},{6,14},{7,15},{8,0},{9,1},... | collective-permute-start | bytes 786440 | tf_op jit(solution)/shard_map/ppermute | solution.py:36
  218.9 23.3 %collective-permute-start.34 = (bf16[2,128,1024]{2,1,0:T(8,128)(2,1)S(1)}, bf16[2,128,1024]{2,1,0:T(8,128)(2,1)}, u32[]{:S(2)}, u32[]{:S(2)}) collective-permute-start(bf16[2,128,1024]{2,1,0:T(8,128)(2,1)S(1)} %shard_map.92.refs_0_), channel_id=1, source_target_pairs={{0,8},{1,9},{2,10},{3,11},{4,12},{5,13},{6,14},{7,15},{8,0},{9,1},... | collective-permute-start | bytes 1572872 | tf_op jit(solution)/shard_map/ppermute | solution.py:36
  (41 other events, 401.0 us)
